TPU v7x, 512 devices: a whole 4x4x16 slice. The times are simulated.
512 devices in a mesh: band: 32 (over x, z_hi, y), grid: 16 (over z_lo, core).
Axes of the slice: x: 4, y: 4, z: 16 (z_hi: 2, z_lo: 8; z = z_hi * 8 + z_lo), core: 2. Of those that a mesh axis runs over, the one named last changes fastest.
Arguments:
- occupied: float32 [32, 128, 128, 128], P('band', 'grid'), may hold values from -6 to 6
- target_coefficients: float32 [32, 64, 6144], P('band', None, 'grid'), may hold values from -24 to 24
- slot_column: int32 [6144], replicated, may hold values from -1 to 16383, as said below
- column_length: int32 [6144], replicated, may hold values from 0 to 63, as said below
Outputs:
- exchange_out: float32 [32, 128, 128, 128], P('band', 'grid')
Inputs may be any that keep to these rules, and one draw needn't show every extreme that they name: `slot_column`: slot q * 384 + s belongs to grid index q. Every column kx * 128 + ky with freq(kx)^2 + freq(ky)^2 <= 31^2 stands in exactly one slot; each grid index's used slots come first and the rest hold -1; some grid index uses all 384 slots. `column_length`: for a used slot, 1 + 2 h with h the largest integer such that h^2 <= 31^2 - freq(kx)^2 - freq(ky)^2 of its column; 0 for an unused slot.
All inputs are finite; a program needn't handle non-finite values.
Results may differ from a plain program's by a relative error of at most 0.0003.
Values sent between devices are 32-bit elements; how exact they have to be, the bound alone decides.
No kernel may reach another device: no remote copies, remote signals or barrier semaphores. Data moves between devices by JAX's collectives and lax.ppermute only.
A program may use at most 64 MiB of HBM per device.

v0:
```python
import math

import jax
import jax.numpy as jnp
from jax import lax
from jax.sharding import PartitionSpec as P

SHIFTS = 2


THETA = 3.9
EXACT = lax.Precision.HIGHEST


def shifted(value, axis, steps):
    count = lax.axis_size(axis)
    pairs = [(source, (source + steps) % count) for source in range(count)]
    return lax.ppermute(value, axis, pairs)


def cas_table(freq_ids, coord_ids, points):
    phase_int = freq_ids[:, None] * coord_ids[None, :] % points
    angle_rad = phase_int.astype(jnp.float32) * (2.0 * math.pi / points)
    return (jnp.cos(angle_rad) + jnp.sin(angle_rad)) / math.sqrt(points)


def freq_square(index_arr, points):
    folded = jnp.minimum(index_arr, points - index_arr)
    return folded * folded


def kernel_table(square_int, points):
    square = square_int.astype(jnp.float32)
    factor = points**1.5 / 16.0
    safe_sq = jnp.maximum(square, 1.0)
    general = factor * (1.0 - jnp.cos(THETA * jnp.sqrt(safe_sq))) / safe_sq
    kernel_val = jnp.where(square_int == 0, factor * THETA * THETA / 2.0, general)
    return jnp.where(square_int >= (points // 4) ** 2, 0.0, kernel_val)


def per_device(occupied, target_coefficients, slot_column, column_length):
    grid_count = lax.axis_size("grid")
    grid_index = lax.axis_index("grid")
    occ_count = occupied.shape[0]
    slab_depth = occupied.shape[1]
    points = occupied.shape[2]
    tgt_count = target_coefficients.shape[0]
    packed_len = target_coefficients.shape[1]
    slot_cap = target_coefficients.shape[2]
    row_ids = jnp.arange(points, dtype=jnp.int32)
    own_length = lax.dynamic_slice_in_dim(column_length, grid_index * slot_cap, slot_cap)
    packed_ids = jnp.arange(packed_len, dtype=jnp.int32)
    packed_wavevector = jnp.where(
        packed_ids % 2 == 1, (packed_ids + 1) // 2, (points - packed_ids // 2) % points
    )
    live_mask = (packed_ids[:, None] < own_length[None, :]).astype(jnp.float32)
    depth_table = cas_table(packed_wavevector, row_ids, points)
    column_lines = jnp.einsum(
        "tpc,pr->trc", target_coefficients * live_mask[None], depth_table, precision=EXACT
    )
    slab_columns = lax.all_to_all(column_lines, "grid", split_axis=1, concat_axis=2, tiled=True)
    target_of_slot = jnp.where(slot_column >= 0, slot_column, points * points)
    spectrum = jnp.zeros((tgt_count, slab_depth, points * points), jnp.float32)
    spectrum = spectrum.at[:, :, target_of_slot].add(slab_columns, mode="drop")
    spectrum = spectrum.reshape(tgt_count, slab_depth, points, points)
    plane_table = cas_table(row_ids, row_ids, points)
    target_real = jnp.einsum("tzab,ax->tzxb", spectrum, plane_table, precision=EXACT)
    target_real = jnp.einsum("tzxb,by->tzxy", target_real, plane_table, precision=EXACT)
    kept_ids = jnp.arange(points // 2, dtype=jnp.int32)
    kept_freq = jnp.where(kept_ids <= points // 4, kept_ids, points // 2 + kept_ids)
    kept_count = kept_freq.shape[0]
    local_count = kept_count // grid_count
    plane_basis = cas_table(row_ids, kept_freq, points)
    depth_basis = cas_table(row_ids, kept_freq, points)
    own_freq = lax.dynamic_slice_in_dim(kept_freq, grid_index * local_count, local_count)
    column_square = (
        freq_square(own_freq, points)[:, None] + freq_square(kept_freq, points)[None, :]
    ).reshape(1, -1)
    kernel = kernel_table(freq_square(kept_freq, points)[:, None] + column_square, points)
    pair_count = occ_count * tgt_count

    def solve_pencils(pencil_cols):
        scaled = jnp.einsum("prc,rk->pkc", pencil_cols, depth_basis, precision=EXACT) * kernel[None]
        returned = jnp.einsum("pkc,rk->prc", scaled, depth_basis, precision=EXACT)
        return lax.all_to_all(returned, "grid", split_axis=1, concat_axis=2, tiled=True)

    def potentials(occ_block):
        pair_density = (occ_block[:, None] * target_real[None]).reshape(
            pair_count, slab_depth, points, points
        )
        transformed = jnp.einsum("pzxy,xa->pzay", pair_density, plane_basis, precision=EXACT)
        transformed = jnp.einsum("pzay,yb->pzab", transformed, plane_basis, precision=EXACT)
        transformed = transformed.reshape(pair_count, slab_depth, kept_count * kept_count)
        returned = solve_pencils(
            lax.all_to_all(transformed, "grid", split_axis=2, concat_axis=1, tiled=True)
        )
        returned = returned.reshape(pair_count, slab_depth, kept_count, kept_count)
        potential = jnp.einsum("pzab,xa->pzxb", returned, plane_basis, precision=EXACT)
        potential = jnp.einsum("pzxb,yb->pzxy", potential, plane_basis, precision=EXACT)
        potential = potential.reshape(occ_count, tgt_count, slab_depth, points, points)
        return -jnp.sum(occ_block[:, None] * potential, axis=0)

    accum_out = potentials(occupied)
    carried = occupied
    for shift_index in range(SHIFTS):
        carried = shifted(carried, "band", 1)
        accum_out = accum_out + potentials(carried)
    return accum_out


def solution(mesh):
    placed = (P("band", "grid", None, None), P("band", None, "grid"), P(), P())
    return jax.shard_map(
        per_device,
        mesh=mesh,
        in_specs=placed,
        out_specs=P("band", "grid", None, None),
        check_vma=False,
    )
```

profile of v0, /device:TPU:1, one launch (start us, length us, event | category | flops | bytes accessed | tf_op | source)
XLA Modules:
  0.0 310.5 jit_solution(15551459672511316063)
XLA Ops:
  0.0 0.8 dynamic_slice.6
  0.8 1.4 convolution_bitcast_fusion.4
  2.3 0.9 copy.49
  3.1 14.0 %all-to-all-start = ((f32[1,128,384]{2,0,1:T(1,128)}), f32[1,128,384]{2,0,1:T(1,128)S(1)}, u32[]{:S(2)}, u32[]{:S(2)}) async-start(f32[1,128,384]{2,0,1:T(1,128)} %copy.49), calls=%async_computation | async-start | bytes 393216 | tf_op jit(solution)/shard_map/all_to_all | solution.py:61
  17.2 3.2 %collective-permute-start = (f32[1,8,128,128]{3,2,1,0:T(8,128)}, f32[1,8,128,128]{3,2,1,0:T(8,128)}, u32[]{:S(2)}, u32[]{:S(2)}) collective-permute-start(f32[1,8,128,128]{3,2,1,0:T(8,128)} %param.4), channel_id=1, source_target_pairs={{0,16},{16,32},{32,48},{48,64},{64,80},{80,96},{96,112},{112,128},... | collective-permute-start | bytes 1572872 | tf_op jit(solution)/shard_map/ppermute | solution.py:18
  20.5 0.7 compare_select_fusion
  21.3 24.7 %collective-permute-done = f32[1,8,128,128]{3,2,1,0:T(8,128)} collective-permute-done((f32[1,8,128,128]{3,2,1,0:T(8,128)}, f32[1,8,128,128]{3,2,1,0:T(8,128)}, u32[]{:S(2)}, u32[]{:S(2)}) %collective-permute-start) | collective-permute-done | bytes 524320 | tf_op jit(solution)/shard_map/ppermute | solution.py:18
  46.0 1.9 collective-permute-start.1
  47.9 1.0 copy.50
  49.0 37.1 %scatter_custom_fusion = f32[8,16384]{0,1:T(8,128)} fusion(s32[6144]{0:T(1024)S(1)} %compare_select_fusion, f32[6144,8]{1,0:T(8,128)S(1)} %bitcast.174, f32[]{:T(128)} %constant.109.clone.1), kind=kCustom, calls=%fused_computation.1 | custom fusion | flops 49152 | bytes 524292 | tf_op jit(solution)/shard_map/scatter-add | solution.py:64
  86.1 5.2 %copy.52 = f32[8,128,128]{2,1,0:T(8,128)S(1)} copy(f32[8,128,128]{0,2,1:T(8,128)} %bitcast.167) | data formatting | bytes 1048576 | tf_op jit(solution)/shard_map/reshape.3
  91.3 0.9 convolution_bitcast_fusion
  92.2 0.8 fusion.28
  93.0 0.6 convolution_bitcast_fusion.3
  94.2 0.6 copy.73
  95.4 19.3 %reduce = f32[4096,8]{1,0:T(8,128)} reduce(f32[4096,1,8]{2,1,0:T(1,128)S(1)} %bitcast.168, f32[]{:T(128)} %broadcast.373), dimensions={1}, to_apply=%bitcast.144.reduce_sub_computation | reduce | bytes 262148
  114.7 3.3 %reshape.325 = f32[16,1,2048]{2,1,0:T(1,128)} reshape(f32[4096,8]{1,0:T(8,128)} %reduce) | data formatting | bytes 262144
  118.0 47.0 %all-to-all-start.1 = ((f32[16,1,2048]{2,1,0:T(1,128)}), f32[16,1,2048]{2,1,0:T(1,128)S(1)}, u32[]{:S(2)}, u32[]{:S(2)}) async-start(f32[16,1,2048]{2,1,0:T(1,128)} %reshape.325), calls=%async_computation.1 | async-start | bytes 262144 | tf_op jit(solution)/shard_map/all_to_all | solution.py:95
  165.0 1.7 convolution_bitcast_fusion.2
  167.2 0.6 copy.75
  167.9 19.3 %reduce.2 = f32[4096,8]{1,0:T(8,128)} reduce(f32[4096,1,8]{2,1,0:T(1,128)S(1)} %bitcast.169, f32[]{:T(128)} %broadcast.373), dimensions={1}, to_apply=%bitcast.146.reduce_sub_computation | reduce | bytes 262148
  187.2 3.3 %reshape.327 = f32[16,1,2048]{2,1,0:T(1,128)} reshape(f32[4096,8]{1,0:T(8,128)} %reduce.2) | data formatting | bytes 262144
  190.5 10.3 %all-to-all-start.3 = ((f32[16,1,2048]{2,1,0:T(1,128)}), f32[16,1,2048]{2,1,0:T(1,128)S(1)}, u32[]{:S(2)}, u32[]{:S(2)}) async-start(f32[16,1,2048]{2,1,0:T(1,128)} %reshape.327), calls=%async_computation.3 | async-start | bytes 262144 | tf_op jit(solution)/shard_map/all_to_all | solution.py:95
  200.8 1.7 convolution_bitcast_fusion.1
  203.0 0.6 copy.77
  203.7 19.3 %reduce.4 = f32[4096,8]{1,0:T(8,128)} reduce(f32[4096,1,8]{2,1,0:T(1,128)S(1)} %bitcast.170, f32[]{:T(128)} %broadcast.373), dimensions={1}, to_apply=%bitcast.148.reduce_sub_computation | reduce | bytes 262148
  223.0 3.3 %reshape.329 = f32[16,1,2048]{2,1,0:T(1,128)} reshape(f32[4096,8]{1,0:T(8,128)} %reduce.4) | data formatting | bytes 262144
  226.3 10.5 %all-to-all-start.5 = ((f32[16,1,2048]{2,1,0:T(1,128)}), f32[16,1,2048]{2,1,0:T(1,128)S(1)}, u32[]{:S(2)}, u32[]{:S(2)}) async-start(f32[16,1,2048]{2,1,0:T(1,128)} %reshape.329), calls=%async_computation.5 | async-start | bytes 262144 | tf_op jit(solution)/shard_map/all_to_all | solution.py:95
  237.0 0.9 reduce.1
  237.8 3.5 %reshape.326 = f32[4096,1,8]{2,1,0:T(1,128)S(1)} reshape(f32[16,2048]{1,0:T(8,128)S(1)} %reduce.1) | data formatting | bytes 262144
  241.3 0.6 copy.74
  243.0 0.8 copy.56
  243.8 0.9 reduce.3
  244.7 3.5 %reshape.328 = f32[4096,1,8]{2,1,0:T(1,128)S(1)} reshape(f32[16,2048]{1,0:T(8,128)S(1)} %reduce.3) | data formatting | bytes 262144
  248.2 0.6 copy.76
  248.8 10.2 %all-to-all-start.2 = ((f32[1,128,256]{2,0,1:T(1,128)}), f32[1,128,256]{2,0,1:T(1,128)S(1)}, u32[]{:S(2)}, u32[]{:S(2)}) async-start(f32[1,128,256]{2,0,1:T(1,128)} %copy.56), calls=%async_computation.2 | async-start | bytes 262144 | tf_op jit(solution)/shard_map/all_to_all | solution.py:85
  260.1 0.8 copy.62
  260.9 0.9 reduce.5
  261.7 3.5 %reshape.330 = f32[4096,1,8]{2,1,0:T(1,128)S(1)} reshape(f32[16,2048]{1,0:T(8,128)S(1)} %reduce.5) | data formatting | bytes 262144
  266.9 0.8 copy.68
  267.7 3.2 %all-to-all-done.2 = f32[1,128,256]{2,0,1:T(1,128)S(1)} async-done(((f32[1,128,256]{2,0,1:T(1,128)}), f32[1,128,256]{2,0,1:T(1,128)S(1)}, u32[]{:S(2)}, u32[]{:S(2)}) %all-to-all-start.2) | async-done | bytes 131104 | tf_op jit(solution)/shard_map/all_to_all | solution.py:85
  270.9 6.7 %all-to-all-start.4 = ((f32[1,128,256]{2,0,1:T(1,128)}), f32[1,128,256]{2,0,1:T(1,128)S(1)}, u32[]{:S(2)}, u32[]{:S(2)}) async-start(f32[1,128,256]{2,0,1:T(1,128)} %copy.62), calls=%async_computation.4 | async-start | bytes 262144 | tf_op jit(solution)/shard_map/all_to_all | solution.py:85
  278.5 1.0 fusion.4
  279.5 10.1 %all-to-all-done.4 = f32[1,128,256]{2,0,1:T(1,128)S(1)} async-done(((f32[1,128,256]{2,0,1:T(1,128)}), f32[1,128,256]{2,0,1:T(1,128)S(1)}, u32[]{:S(2)}, u32[]{:S(2)}) %all-to-all-start.4) | async-done | bytes 131104 | tf_op jit(solution)/shard_map/all_to_all | solution.py:85
  289.6 4.9 %all-to-all-start.6 = ((f32[1,128,256]{2,0,1:T(1,128)}), f32[1,128,256]{2,0,1:T(1,128)S(1)}, u32[]{:S(2)}, u32[]{:S(2)}) async-start(f32[1,128,256]{2,0,1:T(1,128)} %copy.68), calls=%async_computation.6 | async-start | bytes 262144 | tf_op jit(solution)/shard_map/all_to_all | solution.py:85
  295.5 2.1 fusion.5
  297.6 9.1 %all-to-all-done.6 = f32[1,128,256]{2,0,1:T(1,128)S(1)} async-done(((f32[1,128,256]{2,0,1:T(1,128)}), f32[1,128,256]{2,0,1:T(1,128)S(1)}, u32[]{:S(2)}, u32[]{:S(2)}) %all-to-all-start.6) | async-done | bytes 131104 | tf_op jit(solution)/shard_map/all_to_all | solution.py:85
  307.5 2.9 fusion.7
  (36 shorter events, 8.7 us)
Async XLA Ops:
  3.1 44.8 %all-to-all-start = ((f32[1,128,384]{2,0,1:T(1,128)}), f32[1,128,384]{2,0,1:T(1,128)S(1)}, u32[]{:S(2)}, u32[]{:S(2)}) async-start(f32[1,128,384]{2,0,1:T(1,128)} %copy.49), calls=%async_computation | async-start | bytes 393216 | tf_op jit(solution)/shard_map/all_to_all | solution.py:61
  17.2 28.8 %collective-permute-start = (f32[1,8,128,128]{3,2,1,0:T(8,128)}, f32[1,8,128,128]{3,2,1,0:T(8,128)}, u32[]{:S(2)}, u32[]{:S(2)}) collective-permute-start(f32[1,8,128,128]{3,2,1,0:T(8,128)} %param.4), channel_id=1, source_target_pairs={{0,16},{16,32},{32,48},{48,64},{64,80},{80,96},{96,112},{112,128},... | collective-permute-start | bytes 1572872 | tf_op jit(solution)/shard_map/ppermute | solution.py:18
  46.0 154.8 %collective-permute-start.1 = (f32[1,8,128,128]{3,2,1,0:T(8,128)}, f32[1,8,128,128]{3,2,1,0:T(8,128)}, u32[]{:S(2)}, u32[]{:S(2)}) collective-permute-start(f32[1,8,128,128]{3,2,1,0:T(8,128)} %collective-permute-done), channel_id=1, source_target_pairs={{0,16},{16,32},{32,48},{48,64},{64,80},{80,96},{96,112},{112,128},... | collective-permute-start | bytes 1572872 | tf_op jit(solution)/shard_map/ppermute | solution.py:18
  86.1 7.0 %copy-start = (f32[1,8,128,128]{3,2,1,0:T(8,128)S(1)}, f32[1,8,128,128]{3,2,1,0:T(8,128)}, u32[]{:S(2)}) copy-start(f32[1,8,128,128]{3,2,1,0:T(8,128)} %param.4) | copy-start | bytes 1572868
  118.0 72.5 %all-to-all-start.1 = ((f32[16,1,2048]{2,1,0:T(1,128)}), f32[16,1,2048]{2,1,0:T(1,128)S(1)}, u32[]{:S(2)}, u32[]{:S(2)}) async-start(f32[16,1,2048]{2,1,0:T(1,128)} %reshape.325), calls=%async_computation.1 | async-start | bytes 262144 | tf_op jit(solution)/shard_map/all_to_all | solution.py:95
  190.5 35.8 %all-to-all-start.3 = ((f32[16,1,2048]{2,1,0:T(1,128)}), f32[16,1,2048]{2,1,0:T(1,128)S(1)}, u32[]{:S(2)}, u32[]{:S(2)}) async-start(f32[16,1,2048]{2,1,0:T(1,128)} %reshape.327), calls=%async_computation.3 | async-start | bytes 262144 | tf_op jit(solution)/shard_map/all_to_all | solution.py:95
  226.3 22.5 %all-to-all-start.5 = ((f32[16,1,2048]{2,1,0:T(1,128)}), f32[16,1,2048]{2,1,0:T(1,128)S(1)}, u32[]{:S(2)}, u32[]{:S(2)}) async-start(f32[16,1,2048]{2,1,0:T(1,128)} %reshape.329), calls=%async_computation.5 | async-start | bytes 262144 | tf_op jit(solution)/shard_map/all_to_all | solution.py:95
  248.8 22.1 %all-to-all-start.2 = ((f32[1,128,256]{2,0,1:T(1,128)}), f32[1,128,256]{2,0,1:T(1,128)S(1)}, u32[]{:S(2)}, u32[]{:S(2)}) async-start(f32[1,128,256]{2,0,1:T(1,128)} %copy.56), calls=%async_computation.2 | async-start | bytes 262144 | tf_op jit(solution)/shard_map/all_to_all | solution.py:85
  270.9 18.7 %all-to-all-start.4 = ((f32[1,128,256]{2,0,1:T(1,128)}), f32[1,128,256]{2,0,1:T(1,128)S(1)}, u32[]{:S(2)}, u32[]{:S(2)}) async-start(f32[1,128,256]{2,0,1:T(1,128)} %copy.62), calls=%async_computation.4 | async-start | bytes 262144 | tf_op jit(solution)/shard_map/all_to_all | solution.py:85
  289.6 17.0 %all-to-all-start.6 = ((f32[1,128,256]{2,0,1:T(1,128)}), f32[1,128,256]{2,0,1:T(1,128)S(1)}, u32[]{:S(2)}, u32[]{:S(2)}) async-start(f32[1,128,256]{2,0,1:T(1,128)} %copy.68), calls=%async_computation.6 | async-start | bytes 262144 | tf_op jit(solution)/shard_map/all_to_all | solution.py:85
where the time goes:
time: 316 us; the launch traced here: 311 us
  starting transfers between devices  109 us (34%)
  other arithmetic  98.5 us (31%)
  waiting for transfers between devices  47.1 us (15%)
  local copies, waits for them, and re-layouts  35.9 us (11%)
  matrix products  19.7 us (6%)
    all_to_all x3, starting transfers between devices, potentials(): lax.all_to_all(transformed, 'grid', split_axis=2, concat_axis=1, tiled=True)  67.7 us
    unnamed x3, other arithmetic  57.9 us
    scatter-add x1, other arithmetic, per_device(): spectrum = spectrum.at[:, :, target_of_slot].add(slab_columns, mode='drop')  37.1 us
    ppermute x2, waiting for transfers between devices, shifted(): return lax.ppermute(value, axis, pairs)  24.7 us
    all_to_all x3, waiting for transfers between devices, solve_pencils(): lax.all_to_all(returned, 'grid', split_axis=1, concat_axis=2, tiled=True)  22.4 us
    all_to_all x3, starting transfers between devices, solve_pencils(): lax.all_to_all(returned, 'grid', split_axis=1, concat_axis=2, tiled=True)  21.9 us
    unnamed x9, local copies, waits for them, and re-layouts  21.1 us
    all_to_all x1, starting transfers between devices, per_device(): lax.all_to_all(column_lines, 'grid', split_axis=1, concat_axis=2, tiled=T...  14 us
  transfers between devices with their start and end apart: 9, of which 4 were waited for; matrix products, arithmetic and copies ran while one was open for 47% of the time, Pallas kernels for 0%

commit v1 on v0

v1 whole, which is shorter than its diff:
```python
import functools
import math

import jax
import jax.numpy as jnp
import ml_dtypes
import numpy as np
from jax import lax
from jax.experimental import pallas as pl
from jax.experimental.pallas import tpu as pltpu
from jax.sharding import PartitionSpec as P

THETA = 3.9
N = 128
K = 64
GRID = 16
SLAB = N // GRID
OWN = K // GRID
CAP = 384
f32, bf16 = jnp.float32, jnp.bfloat16


def cas(freq, coord):
    phase = (np.asarray(freq)[:, None] * np.asarray(coord)[None, :]) % N
    angle = phase * (2.0 * math.pi / N)
    return (np.cos(angle) + np.sin(angle)) / math.sqrt(N)


def halves(table):
    table = np.asarray(table, np.float32)
    high = table.astype(ml_dtypes.bfloat16)
    low = (table - high.astype(np.float32)).astype(ml_dtypes.bfloat16)
    return np.stack([high, low])


def tables():
    points = np.arange(N)
    kept = np.arange(K)
    kept = np.where(kept <= N // 4, kept, kept + K)
    packed = np.arange(K)
    packed_freq = np.where(packed % 2 == 1, (packed + 1) // 2, (N - packed // 2) % N)
    basis = cas(kept, points)
    order = np.arange(K).reshape(GRID, OWN).T.reshape(-1)
    square = np.minimum(kept, N - kept) ** 2
    total = square[:, None, None] + square[None, :, None] + square[None, None, :]
    factor = N**1.5 / 16.0
    safe = np.maximum(total, 1)
    kernel = np.where(total == 0, factor * THETA * THETA / 2.0, factor * (1.0 - np.cos(THETA * np.sqrt(safe))) / safe)
    kernel = np.where(total >= (N // 4) ** 2, 0.0, kernel)
    kernel = kernel.reshape(K, GRID, OWN * K).transpose(1, 0, 2)
    zero = np.zeros((K, N))
    return dict(
        pack=halves(cas(packed_freq, points).T),
        twice=halves(np.concatenate([basis.T, basis.T], 1)),
        rows=halves(basis[order]),
        cols=halves(basis[order].T),
        diag=halves(np.block([[basis, zero], [zero, basis]])),
        depth=halves(basis),
        depth_t=halves(basis.T),
        kernel=kernel.astype(np.float32),
    )


def split(value):
    high = value.astype(bf16)
    return high, (value - high.astype(f32)).astype(bf16)


def mul(a, b):
    return jnp.dot(a, b, preferred_element_type=f32)


def right(value, table):
    high, low = split(value)
    return mul(high, table[0]) + mul(low, table[0]) + mul(high, table[1])


def left(table, value):
    high, low = split(value)
    return mul(table[0], high) + mul(table[0], low) + mul(table[1], high)


def forward(pair, store, twice, rows):
    first = right(pair.reshape(SLAB * N, N), twice)
    lane = lax.broadcasted_iota(jnp.int32, (GRID, N), 1) < K
    for z in range(SLAB):
        both = left(rows, first[z * N : (z + 1) * N])
        part = [both[low * GRID : (low + 1) * GRID] for low in range(OWN)]
        store(z, 0, jnp.where(lane, part[0], part[1]))
        store(z, 1, jnp.where(lane, part[2], part[3]))


def backward(spectrum, diag, cols):
    part = []
    for half in range(2):
        lines = right(spectrum[half], diag)
        part += [lines[:, :N], lines[:, N:]]
    out = []
    for z in range(SLAB):
        stacked = jnp.concatenate([p[z * GRID : (z + 1) * GRID] for p in part], 0)
        out.append(left(cols, stacked))
    return out


def lines_kernel(index_ref, coef_ref, length_ref, pack, out_ref):
    start = index_ref[0] * (CAP // N)
    entry = lax.broadcasted_iota(jnp.int32, (K, N), 0)
    for j in range(CAP // N):
        length = length_ref[pl.ds(start + j, 1), :]
        live = jnp.where(entry < length, coef_ref[:, j * N : (j + 1) * N], 0.0)
        out_ref[:, j * N : (j + 1) * N] = left(pack, live)


def target_kernel(slab_ref, slot_ref, occ_ref, twice, rows, cols, diag, psi_ref, out_ref, values, picks):
    owner = lax.broadcasted_iota(jnp.int32, (GRID, N), 0)
    place = lax.broadcasted_iota(jnp.int32, (OWN * K, N), 0)
    for chunk in range(GRID * CAP // N):
        source, j = divmod(chunk, CAP // N)
        lanes = pl.ds(chunk * N, N)
        slot = slot_ref[pl.ds(chunk, 1), :]
        first = (slot // N) % K
        second = slot % K
        high = jnp.where(slot >= 0, first // OWN, GRID)
        low = (first % OWN) * K + second
        picks[:, lanes] = jnp.where(place == low, 1.0, 0.0).astype(bf16)
        block = slab_ref[source * SLAB : (source + 1) * SLAB, j * N : (j + 1) * N]
        head = block.astype(bf16).astype(f32)
        hit = owner == high
        for piece, part in enumerate((head, block - head)):
            for z in range(SLAB):
                row = (piece * SLAB + z) * GRID
                values[row : row + GRID, lanes] = jnp.where(hit, part[z : z + 1], 0.0).astype(bf16)
    both = lax.dot_general(values[...], picks[...], (((1,), (1,)), ((), ())), preferred_element_type=f32)
    spectrum = both[:N] + both[N:]
    planes = backward([spectrum[:, :N], spectrum[:, N:]], diag, cols)
    for z in range(SLAB):
        psi_ref[z] = planes[z]

    def store(z, half, value):
        out_ref[pl.ds(half * SLAB + z, GRID, stride=2 * SLAB), :] = value

    forward(occ_ref[...] * psi_ref[...], store, twice, rows)


def pair_kernel(psi_ref, *refs):
    *occ_refs, twice, rows, out_ref = refs
    count = len(occ_refs)
    for p, occ_ref in enumerate(occ_refs):

        def store(z, half, value):
            out_ref[pl.ds((2 * p + half) * SLAB + z, GRID, stride=2 * count * SLAB), :] = value

        forward(occ_ref[...] * psi_ref[...], store, twice, rows)


def pencil_kernel(index_ref, in_ref, kernel_ref, depth, depth_t, out_ref):
    weight = kernel_ref[index_ref[0]]
    for k in range(in_ref.shape[1]):
        half = k % 2
        scaled = left(depth, in_ref[:, k].reshape(N, N)) * weight[:, half * N : (half + 1) * N]
        out_ref[:, k] = left(depth_t, scaled).reshape(GRID, SLAB, N)


def apply_kernel(count, *refs):
    in_ref = refs[0]
    occ_refs = refs[1 : 1 + count]
    *base, cols, diag, out_ref = refs[1 + count :]
    for p, occ_ref in enumerate(occ_refs):
        spectrum = [
            jnp.concatenate(
                [
                    in_ref[pl.ds((2 * p + half) * SLAB + z, GRID, stride=2 * count * SLAB), :]
                    for z in range(SLAB)
                ],
                0,
            )
            for half in range(2)
        ]
        planes = backward(spectrum, diag, cols)
        for z in range(SLAB):
            old = out_ref[z] if p else (base[0][z] if base else 0.0)
            out_ref[z] = old - occ_ref[z] * planes[z]


PARAMS = pltpu.CompilerParams(vmem_limit_bytes=40 * 2**20)
VM = pl.BlockSpec(memory_space=pltpu.VMEM)
SM = pl.BlockSpec(memory_space=pltpu.SMEM)


def call(kernel, shapes, ins, scalar=False, scratch=()):
    many = isinstance(shapes, list)
    return pl.pallas_call(
        kernel,
        out_shape=tuple(jax.ShapeDtypeStruct(s, f32) for s in shapes) if many else jax.ShapeDtypeStruct(shapes, f32),
        in_specs=[SM if scalar and k == 0 else VM for k in range(len(ins))],
        out_specs=tuple(VM for _ in shapes) if many else VM,
        scratch_shapes=scratch,
        compiler_params=PARAMS,
    )(*ins)


def exchange(value):
    return lax.all_to_all(value, "grid", split_axis=0, concat_axis=0, tiled=True)


def per_device(occupied, coefficients, slot_column, column_length):
    tab = {name: jnp.asarray(value) for name, value in tables().items()}
    index = lax.axis_index("grid").astype(jnp.int32).reshape(1)
    occ = occupied.reshape(SLAB, N, N)
    ring = lax.axis_size("band")

    def shifted(value, steps):
        return lax.ppermute(value, "band", [(s, (s + steps) % ring) for s in range(ring)])

    occ1 = shifted(occ, 1)
    occ2 = shifted(occ, 2)

    lines = call(
        lines_kernel,
        (N, CAP),
        (index, coefficients.reshape(K, CAP), column_length.reshape(-1, N), tab["pack"]),
        scalar=True,
    )
    slab = exchange(lines.reshape(GRID, SLAB, CAP)).reshape(N, CAP)
    psi, sent = call(
        target_kernel,
        [(SLAB, N, N), (2 * N, N)],
        (slab, slot_column.reshape(-1, N), occ, tab["twice"], tab["rows"], tab["cols"], tab["diag"]),
        scratch=(pltpu.VMEM((2 * N, GRID * CAP), bf16), pltpu.VMEM((OWN * K, GRID * CAP), bf16)),
    )

    def solve(value, count):
        value = exchange(value.reshape(GRID, 2 * count * SLAB, N))
        value = call(
            pencil_kernel,
            (GRID, 2 * count, SLAB, N),
            (index, value.reshape(GRID, 2 * count, SLAB, N), tab["kernel"], tab["depth"], tab["depth_t"]),
            scalar=True,
        )
        value = exchange(value.reshape(GRID, 2 * count * SLAB, N))
        return value.reshape(GRID * 2 * count * SLAB, N)

    out = call(
        functools.partial(apply_kernel, 1), (SLAB, N, N), (solve(sent, 1), occ, tab["cols"], tab["diag"])
    )
    sent = call(pair_kernel, (4 * N, N), (psi, occ1, occ2, tab["twice"], tab["rows"]))
    out = call(
        functools.partial(apply_kernel, 2),
        (SLAB, N, N),
        (solve(sent, 2), occ1, occ2, out, tab["cols"], tab["diag"]),
    )
    return out.reshape(1, SLAB, N, N)


def solution(mesh):
    placed = (P("band", "grid", None, None), P("band", None, "grid"), P(), P())
    return jax.shard_map(
        per_device,
        mesh=mesh,
        in_specs=placed,
        out_specs=P("band", "grid", None, None),
        check_vma=False,
    )
```

time: 316 us -> 207 us (0.66)
  the two profiles are of different devices: /device:TPU:1 before, /device:TPU:25 now
where the time goes in v1:
time: 207 us; the launch traced here: 206 us
  starting transfers between devices  108 us (52%)
  waiting for transfers between devices  78.7 us (38%)
  Pallas kernels  13.4 us (6%)
  local copies, waits for them, and re-layouts  5.88 us (3%)
    all_to_all x5, starting transfers between devices, exchange(): lax.all_to_all(value, 'grid', split_axis=0, concat_axis=0, tiled=True)  95.7 us
    all_to_all x5, waiting for transfers between devices, exchange(): lax.all_to_all(value, 'grid', split_axis=0, concat_axis=0, tiled=True)  78.7 us
    pallas_call x7, Pallas kernels, call(): pl.pallas_call(kernel, out_shape=tuple((jax.ShapeDtypeStruct(s, f32) for...  13.4 us
    ppermute x2, starting transfers between devices, shifted(): lax.ppermute(value, 'band', [(s, (s + steps) % ring) for s in range(ring)])  11.8 us
    unnamed x30, local copies, waits for them, and re-layouts  5.88 us
  transfers between devices with their start and end apart: 7, of which 5 were waited for; matrix products, arithmetic and copies ran while one was open for 0% of the time, Pallas kernels for 5%

profile of v1, /device:TPU:25, one launch (start us, length us, event | category | flops | bytes accessed | tf_op | source)
XLA Modules:
  0.0 205.6 jit_solution(3197528609386916716)
XLA Ops:
  0.0 0.0 copy-start.1
  0.0 0.0 copy-start.11
  0.0 0.9 copy-done.11
  1.0 0.0 copy-start.12
  1.0 0.8 copy-done.12
  1.8 0.0 copy-start.13
  1.8 0.7 copy-done.13
  2.5 0.9 shard_map.118
  3.4 0.0 copy-start.2
  3.4 0.0 copy-start.3
  3.4 0.0 copy-start.7
  3.4 13.3 %all-to-all-start = ((f32[16,8,384]{2,1,0:T(8,128)}), f32[16,8,384]{2,1,0:T(8,128)S(1)}, u32[]{:S(2)}, u32[]{:S(2)}) async-start(f32[16,8,384]{2,1,0:T(8,128)} %bitcast.3), calls=%async_computation | async-start | bytes 393216 | tf_op jit(solution)/shard_map/all_to_all | solution.py:203
  16.8 0.0 copy-done.1
  16.8 7.6 %collective-permute-start = (f32[8,128,128]{2,1,0:T(8,128)S(1)}, f32[8,128,128]{2,1,0:T(8,128)S(1)}, u32[]{:S(2)}, u32[]{:S(2)}) collective-permute-start(f32[8,128,128]{2,1,0:T(8,128)S(1)} %bitcast.16), channel_id=1, source_target_pairs={{0,16},{16,32},{32,48},{48,64},{64,80},{80,96},{96,112},{112,128},... | collective-permute-start | bytes 1572872 | tf_op jit(solution)/shard_map/ppermute | solution.py:213
  24.4 4.2 %collective-permute-start.1 = (f32[8,128,128]{2,1,0:T(8,128)S(1)}, f32[8,128,128]{2,1,0:T(8,128)S(1)}, u32[]{:S(2)}, u32[]{:S(2)}) collective-permute-start(f32[8,128,128]{2,1,0:T(8,128)S(1)} %bitcast.17), channel_id=1, source_target_pairs={{0,32},{16,48},{32,64},{48,80},{64,96},{80,112},{96,128},{112,144}... | collective-permute-start | bytes 1572872 | tf_op jit(solution)/shard_map/ppermute | solution.py:213
  28.6 2.8 %all-to-all-done = f32[16,8,384]{2,1,0:T(8,128)S(1)} async-done(((f32[16,8,384]{2,1,0:T(8,128)}), f32[16,8,384]{2,1,0:T(8,128)S(1)}, u32[]{:S(2)}, u32[]{:S(2)}) %all-to-all-start) | async-done | bytes 196640 | tf_op jit(solution)/shard_map/all_to_all | solution.py:203
  31.5 0.0 copy-done.2
  31.5 0.0 copy-done.3
  31.5 0.0 copy-done.7
  31.5 0.0 copy-start.8
  31.5 0.7 copy-done.8
  32.2 0.0 copy-start.14
  32.2 0.7 copy-done.14
  33.0 5.0 %shard_map.119 = (f32[8,128,128]{2,1,0:T(8,128)S(1)}, f32[256,128]{1,0:T(8,128)}) custom-call(f32[128,384]{1,0:T(8,128)S(1)} %bitcast.22, s32[48,128]{1,0:T(8,128)S(1)} %bitcast.27, f32[8,128,128]{2,1,0:T(8,128)S(1)} %bitcast.18, bf16[2,128,128]{2,1,0:T(8,128)(2,1)S(1)} %copy-done.7, bf16[2,64,128]{2,1,0:T(8,128)(2,1)S(1)} %copy-done.8, ...), custom_call_target="tpu_custom_call" | custom-call | tf_op jit(solution)/shard_map/pallas_call | solution.py:192
  38.0 0.0 copy-start.4
  38.0 0.8 copy-done.4
  38.8 0.0 copy-start.9
  38.8 62.6 %all-to-all-start.3 = ((f32[16,16,128]{2,1,0:T(8,128)}), f32[16,16,128]{2,1,0:T(8,128)S(1)}, u32[]{:S(2)}, u32[]{:S(2)}) async-start(f32[16,16,128]{2,1,0:T(8,128)} %bitcast.11), calls=%async_computation.3 | async-start | bytes 262144 | tf_op jit(solution)/shard_map/all_to_all | solution.py:203
  101.4 0.0 collective-permute-done.refs_0_.refs_1_
  101.4 0.0 collective-permute-done.1.refs_1_.refs_2_
  101.4 0.0 copy-done.9
  101.4 0.0 copy-start.5
  101.4 1.0 copy-done.5
  102.4 2.1 %shard_map.120 = f32[512,128]{1,0:T(8,128)} custom-call(f32[8,128,128]{2,1,0:T(8,128)S(1)} %copy-done.5, f32[8,128,128]{2,1,0:T(8,128)S(1)} %collective-permute-done.refs_0_.refs_1_, f32[8,128,128]{2,1,0:T(8,128)S(1)} %collective-permute-done.1.refs_1_.refs_2_, bf16[2,128,128]{2,1,0:T(8,128)(2,1)S(1)} %copy-done.7, bf16[2,64,128]{2,1,0:T(8,128)(2,1)S(1)} %copy-done.9), custom_call_target="tpu_custom_call" | custom-call | tf_op jit(solution)/shard_map/pallas_call | solution.py:192
  104.5 33.4 %all-to-all-done.3 = f32[16,16,128]{2,1,0:T(8,128)S(1)} async-done(((f32[16,16,128]{2,1,0:T(8,128)}), f32[16,16,128]{2,1,0:T(8,128)S(1)}, u32[]{:S(2)}, u32[]{:S(2)}) %all-to-all-start.3) | async-done | bytes 131104 | tf_op jit(solution)/shard_map/all_to_all | solution.py:203
  137.9 9.6 %all-to-all-start.1 = ((f32[16,32,128]{2,1,0:T(8,128)}), f32[16,32,128]{2,1,0:T(8,128)S(1)}, u32[]{:S(2)}, u32[]{:S(2)}) async-start(f32[16,32,128]{2,1,0:T(8,128)} %bitcast.7), calls=%async_computation.1 | async-start | bytes 524288 | tf_op jit(solution)/shard_map/all_to_all | solution.py:203
  147.5 0.0 copy-done
  147.5 0.0 copy-done.6
  147.5 0.0 copy-done.10
  147.5 1.2 shard_map.122
  148.7 15.8 %all-to-all-done.1 = f32[16,32,128]{2,1,0:T(8,128)S(1)} async-done(((f32[16,32,128]{2,1,0:T(8,128)}), f32[16,32,128]{2,1,0:T(8,128)S(1)}, u32[]{:S(2)}, u32[]{:S(2)}) %all-to-all-start.1) | async-done | bytes 262176 | tf_op jit(solution)/shard_map/all_to_all | solution.py:203
  164.5 5.3 %all-to-all-start.4 = ((f32[16,16,128]{2,1,0:T(8,128)}), f32[16,16,128]{2,1,0:T(8,128)S(1)}, u32[]{:S(2)}, u32[]{:S(2)}) async-start(f32[16,16,128]{2,1,0:T(8,128)} %bitcast.13), calls=%async_computation.4 | async-start | bytes 262144 | tf_op jit(solution)/shard_map/all_to_all | solution.py:203
  169.8 1.7 shard_map.121
  171.5 10.3 %all-to-all-done.4 = f32[16,16,128]{2,1,0:T(8,128)S(1)} async-done(((f32[16,16,128]{2,1,0:T(8,128)}), f32[16,16,128]{2,1,0:T(8,128)S(1)}, u32[]{:S(2)}, u32[]{:S(2)}) %all-to-all-start.4) | async-done | bytes 131104 | tf_op jit(solution)/shard_map/all_to_all | solution.py:203
  181.8 4.9 %all-to-all-start.2 = ((f32[16,32,128]{2,1,0:T(8,128)}), f32[16,32,128]{2,1,0:T(8,128)S(1)}, u32[]{:S(2)}, u32[]{:S(2)}) async-start(f32[16,32,128]{2,1,0:T(8,128)} %bitcast.9), calls=%async_computation.2 | async-start | bytes 524288 | tf_op jit(solution)/shard_map/all_to_all | solution.py:203
  186.7 0.6 shard_map.123.refs_3_
  187.3 16.4 %all-to-all-done.2 = f32[16,32,128]{2,1,0:T(8,128)S(1)} async-done(((f32[16,32,128]{2,1,0:T(8,128)}), f32[16,32,128]{2,1,0:T(8,128)S(1)}, u32[]{:S(2)}, u32[]{:S(2)}) %all-to-all-start.2) | async-done | bytes 262176 | tf_op jit(solution)/shard_map/all_to_all | solution.py:203
  203.8 1.8 shard_map.124
  (3 shorter events, 0.0 us)
Async XLA Ops:
  0.0 16.8 %copy-start.1 = (f32[1,8,128,128]{3,2,1,0:T(8,128)S(1)}, f32[1,8,128,128]{3,2,1,0:T(8,128)}, u32[]{:S(2)}) copy-start(f32[1,8,128,128]{3,2,1,0:T(8,128)} %param.12) | copy-start | bytes 1572868
  0.0 1.0 copy-start.11
  1.0 0.8 copy-start.12
  1.8 0.7 copy-start.13
  3.4 28.0 %copy-start.2 = (bf16[2,128,256]{2,1,0:T(8,128)(2,1)S(1)}, bf16[2,128,256]{2,1,0:T(8,128)(2,1)}, u32[]{:S(2)}) copy-start(bf16[2,128,256]{2,1,0:T(8,128)(2,1)} %constant.24.clone.diag.refs_3_.refs_5_) | copy-start | bytes 393220
  3.4 28.0 %copy-start.3 = (bf16[2,128,64]{2,1,0:T(8,128)(2,1)S(1)}, bf16[2,128,64]{2,1,0:T(8,128)(2,1)}, u32[]{:S(2)}) copy-start(bf16[2,128,64]{2,1,0:T(8,128)(2,1)} %constant.23.clone.cols.refs_2_.refs_4_) | copy-start | bytes 98308
  3.4 28.0 %copy-start.7 = (bf16[2,128,128]{2,1,0:T(8,128)(2,1)S(1)}, bf16[2,128,128]{2,1,0:T(8,128)(2,1)}, u32[]{:S(2)}) copy-start(bf16[2,128,128]{2,1,0:T(8,128)(2,1)} %constant.21.clone.twice.refs_2_) | copy-start | bytes 196612
  3.4 28.0 %all-to-all-start = ((f32[16,8,384]{2,1,0:T(8,128)}), f32[16,8,384]{2,1,0:T(8,128)S(1)}, u32[]{:S(2)}, u32[]{:S(2)}) async-start(f32[16,8,384]{2,1,0:T(8,128)} %bitcast.3), calls=%async_computation | async-start | bytes 393216 | tf_op jit(solution)/shard_map/all_to_all | solution.py:203
  16.8 84.6 %collective-permute-start = (f32[8,128,128]{2,1,0:T(8,128)S(1)}, f32[8,128,128]{2,1,0:T(8,128)S(1)}, u32[]{:S(2)}, u32[]{:S(2)}) collective-permute-start(f32[8,128,128]{2,1,0:T(8,128)S(1)} %bitcast.16), channel_id=1, source_target_pairs={{0,16},{16,32},{32,48},{48,64},{64,80},{80,96},{96,112},{112,128},... | collective-permute-start | bytes 1572872 | tf_op jit(solution)/shard_map/ppermute | solution.py:213
  24.4 76.9 %collective-permute-start.1 = (f32[8,128,128]{2,1,0:T(8,128)S(1)}, f32[8,128,128]{2,1,0:T(8,128)S(1)}, u32[]{:S(2)}, u32[]{:S(2)}) collective-permute-start(f32[8,128,128]{2,1,0:T(8,128)S(1)} %bitcast.17), channel_id=1, source_target_pairs={{0,32},{16,48},{32,64},{48,80},{64,96},{80,112},{96,128},{112,144}... | collective-permute-start | bytes 1572872 | tf_op jit(solution)/shard_map/ppermute | solution.py:213
  31.5 0.8 copy-start.8
  32.2 0.7 copy-start.14
  38.0 0.8 copy-start.4
  38.8 62.6 %copy-start.9 = (bf16[2,64,128]{2,1,0:T(8,128)(2,1)S(1)}, bf16[2,64,128]{2,1,0:T(8,128)(2,1)}, u32[]{:S(2)}) copy-start(bf16[2,64,128]{2,1,0:T(8,128)(2,1)} %constant.22.clone.rows.refs_3_) | copy-start | bytes 98308
  38.8 99.1 %all-to-all-start.3 = ((f32[16,16,128]{2,1,0:T(8,128)}), f32[16,16,128]{2,1,0:T(8,128)S(1)}, u32[]{:S(2)}, u32[]{:S(2)}) async-start(f32[16,16,128]{2,1,0:T(8,128)} %bitcast.11), calls=%async_computation.3 | async-start | bytes 262144 | tf_op jit(solution)/shard_map/all_to_all | solution.py:203
  101.4 1.0 copy-start.5
  102.4 45.1 %copy-start = (f32[16,64,256]{2,1,0:T(8,128)S(1)}, f32[16,64,256]{2,1,0:T(8,128)}, u32[]{:S(2)}) copy-start(f32[16,64,256]{2,1,0:T(8,128)} %constant.27.clone.kernel_ref) | copy-start | bytes 3145732
  137.9 9.6 %copy-start.6 = (bf16[2,128,64]{2,1,0:T(8,128)(2,1)S(1)}, bf16[2,128,64]{2,1,0:T(8,128)(2,1)}, u32[]{:S(2)}) copy-start(bf16[2,128,64]{2,1,0:T(8,128)(2,1)} %constant.26.clone.depth_t) | copy-start | bytes 98308
  137.9 9.6 %copy-start.10 = (bf16[2,64,128]{2,1,0:T(8,128)(2,1)S(1)}, bf16[2,64,128]{2,1,0:T(8,128)(2,1)}, u32[]{:S(2)}) copy-start(bf16[2,64,128]{2,1,0:T(8,128)(2,1)} %constant.25.clone.depth) | copy-start | bytes 98308
  137.9 26.6 %all-to-all-start.1 = ((f32[16,32,128]{2,1,0:T(8,128)}), f32[16,32,128]{2,1,0:T(8,128)S(1)}, u32[]{:S(2)}, u32[]{:S(2)}) async-start(f32[16,32,128]{2,1,0:T(8,128)} %bitcast.7), calls=%async_computation.1 | async-start | bytes 524288 | tf_op jit(solution)/shard_map/all_to_all | solution.py:203
  164.5 17.3 %all-to-all-start.4 = ((f32[16,16,128]{2,1,0:T(8,128)}), f32[16,16,128]{2,1,0:T(8,128)S(1)}, u32[]{:S(2)}, u32[]{:S(2)}) async-start(f32[16,16,128]{2,1,0:T(8,128)} %bitcast.13), calls=%async_computation.4 | async-start | bytes 262144 | tf_op jit(solution)/shard_map/all_to_all | solution.py:203
  181.8 21.9 %all-to-all-start.2 = ((f32[16,32,128]{2,1,0:T(8,128)}), f32[16,32,128]{2,1,0:T(8,128)S(1)}, u32[]{:S(2)}, u32[]{:S(2)}) async-start(f32[16,32,128]{2,1,0:T(8,128)} %bitcast.9), calls=%async_computation.2 | async-start | bytes 524288 | tf_op jit(solution)/shard_map/all_to_all | solution.py:203

commit v2 on v1

v2 whole, which is shorter than its diff:
```python
import functools
import itertools
import math

import jax
import jax.numpy as jnp
import ml_dtypes
import numpy as np
from jax import lax
from jax.experimental import pallas as pl
from jax.experimental.pallas import tpu as pltpu
from jax.sharding import PartitionSpec as P

THETA = 3.9
N = 128
K = 64
GRID = 16
SLAB = N // GRID
OWN = K // GRID
CAP = 384
LINE = 4
RING = 16
f32, bf16 = jnp.float32, jnp.bfloat16
SHAPES = dict(
    pack=(N, K), twice=(N, N), rows=(K, N), cols=(N, K), diag=(2 * N, N), depth=(K, N), depth_t=(N, K)
)


def cas(freq, coord):
    phase = (np.asarray(freq)[:, None] * np.asarray(coord)[None, :]) % N
    angle = phase * (2.0 * math.pi / N)
    return (np.cos(angle) + np.sin(angle)) / math.sqrt(N)


def halves(table):
    table = np.asarray(table, np.float32)
    high = table.astype(ml_dtypes.bfloat16)
    low = (table - high.astype(np.float32)).astype(ml_dtypes.bfloat16)
    return np.stack([high, low])


def tables():
    points = np.arange(N)
    kept = np.arange(K)
    kept = np.where(kept <= N // 4, kept, kept + K)
    packed = np.arange(K)
    packed_freq = np.where(packed % 2 == 1, (packed + 1) // 2, (N - packed // 2) % N)
    basis = cas(kept, points)
    order = np.arange(K).reshape(GRID, OWN).T.reshape(-1)
    square = np.minimum(kept, N - kept) ** 2
    total = square[:, None, None] + square[None, :, None] + square[None, None, :]
    factor = N**1.5 / 16.0
    safe = np.maximum(total, 1)
    kernel = np.where(total == 0, factor * THETA * THETA / 2.0, factor * (1.0 - np.cos(THETA * np.sqrt(safe))) / safe)
    kernel = np.where(total >= (N // 4) ** 2, 0.0, kernel)
    kernel = kernel.reshape(K, GRID, OWN * K).transpose(1, 0, 2)
    zero = np.zeros((K, N))
    named = dict(
        pack=cas(packed_freq, points).T,
        twice=np.concatenate([basis.T, basis.T], 1),
        rows=basis[order],
        cols=basis[order].T,
        diag=np.concatenate([np.block([[basis], [zero]]), np.block([[zero], [basis]])]),
        depth=basis,
        depth_t=basis.T,
    )
    assert {name: table.shape for name, table in named.items()} == SHAPES
    base = np.concatenate([np.pad(t, ((0, 0), (0, N - t.shape[1]))) for t in named.values()])
    return halves(base), kernel.astype(np.float32)


def view(base, name):
    start = 0
    for other, (height, width) in SHAPES.items():
        if other == name:
            return [base[h, start : start + height, :width] for h in range(2)]
        start += height
    raise KeyError(name)


def split(value):
    high = value.astype(bf16)
    return high, (value - high.astype(f32)).astype(bf16)


def mul(a, b):
    return jnp.dot(a, b, preferred_element_type=f32)


def right(value, table):
    high, low = split(value)
    return mul(high, table[0]) + mul(low, table[0]) + mul(high, table[1])


def left(table, value):
    high, low = split(value)
    return mul(table[0], high) + mul(table[0], low) + mul(table[1], high)


def forward(pair, store, base):
    twice, rows = view(base, "twice"), view(base, "rows")
    first = right(pair.reshape(SLAB * N, N), twice)
    lane = lax.broadcasted_iota(jnp.int32, (GRID, N), 1) < K
    for z in range(SLAB):
        both = left(rows, first[z * N : (z + 1) * N])
        part = [both[low * GRID : (low + 1) * GRID] for low in range(OWN)]
        store(z, 0, jnp.where(lane, part[0], part[1]))
        store(z, 1, jnp.where(lane, part[2], part[3]))


def backward(spectrum, base):
    diag, cols = view(base, "diag"), view(base, "cols")
    part = []
    for half in range(2):
        part += [right(spectrum[half], [h[low * N : (low + 1) * N] for h in diag]) for low in range(2)]
    out = []
    for z in range(SLAB):
        stacked = jnp.concatenate([p[z * GRID : (z + 1) * GRID] for p in part], 0)
        out.append(left(cols, stacked))
    return out


def lines_kernel(index_ref, coef_ref, length_ref, base, after, out_ref):
    pack = view(base, "pack")
    start = index_ref[0] * (CAP // N)
    entry = lax.broadcasted_iota(jnp.int32, (K, N), 0)
    for j in range(CAP // N):
        length = length_ref[pl.ds(start + j, 1), :]
        live = jnp.where(entry < length, coef_ref[:, j * N : (j + 1) * N], 0.0)
        out_ref[:, j * N : (j + 1) * N] = left(pack, live)


def target_kernel(slab_ref, slot_ref, occ_ref, base, after, psi_ref, out_ref, values, picks):
    owner = lax.broadcasted_iota(jnp.int32, (GRID, N), 0)
    place = lax.broadcasted_iota(jnp.int32, (OWN * K, N), 0)
    for chunk in range(GRID * CAP // N):
        source, j = divmod(chunk, CAP // N)
        lanes = pl.ds(chunk * N, N)
        slot = slot_ref[pl.ds(chunk, 1), :]
        first = (slot // N) % K
        second = slot % K
        high = jnp.where(slot >= 0, first // OWN, GRID)
        low = (first % OWN) * K + second
        picks[:, lanes] = jnp.where(place == low, 1.0, 0.0).astype(bf16)
        block = slab_ref[source * SLAB : (source + 1) * SLAB, j * N : (j + 1) * N]
        head = block.astype(bf16).astype(f32)
        hit = owner == high
        for piece, part in enumerate((head, block - head)):
            for z in range(SLAB):
                row = (piece * SLAB + z) * GRID
                values[row : row + GRID, lanes] = jnp.where(hit, part[z : z + 1], 0.0).astype(bf16)
    both = lax.dot_general(values[...], picks[...], (((1,), (1,)), ((), ())), preferred_element_type=f32)
    spectrum = both[:N] + both[N:]
    planes = backward([spectrum[:, :N], spectrum[:, N:]], base)
    for z in range(SLAB):
        psi_ref[z] = planes[z]

    def store(z, half, value):
        out_ref[pl.ds(half * SLAB + z, GRID, stride=2 * SLAB), :] = value

    forward(occ_ref[...] * psi_ref[...], store, base)


def swap_kernel(step_ref, near, back, after, out_ref):
    out_ref[...] = jnp.where(step_ref[0] == 0, near[...], back[...])


def pair_kernel(step_ref, psi_ref, one, two, near, far, back, swap, own_ref, base, out_ref, occ_ref):
    half = SLAB // 2
    first, second = step_ref[0] == 0, step_ref[0] == 1
    occ_ref[0, :half] = jnp.where(first, near[...], one[:half])
    occ_ref[0, half:] = jnp.where(first, swap[...], one[half:])
    occ_ref[1, :half] = jnp.where(first, far[...], jnp.where(second, swap[...], two[:half]))
    occ_ref[1, half:] = jnp.where(first | second, back[...], two[half:])
    count = occ_ref.shape[0]
    blocks = 2 + 2 * count
    for k in range(2):
        for owner in range(GRID):
            out_ref[pl.ds((owner * blocks + k) * SLAB, SLAB), :] = own_ref[pl.ds((owner * 2 + k) * SLAB, SLAB), :]
    for p in range(count):

        def store(z, half, value):
            out_ref[pl.ds((2 + 2 * p + half) * SLAB + z, GRID, stride=blocks * SLAB), :] = value

        forward(occ_ref[p] * psi_ref[...], store, base)


def pencil_kernel(in_ref, weight, base, out_ref):
    depth, depth_t = view(base, "depth"), view(base, "depth_t")
    for k in range(in_ref.shape[1]):
        half = k % 2
        scaled = left(depth, in_ref[:, k].reshape(N, N)) * weight[:, half * N : (half + 1) * N]
        out_ref[:, k] = left(depth_t, scaled).reshape(GRID, SLAB, N)


def apply_kernel(in_ref, occ_ref, both_ref, base, out_ref):
    count = 1 + both_ref.shape[0]
    blocks = in_ref.shape[0] // (GRID * SLAB)
    for p in range(count):
        spectrum = [
            jnp.concatenate(
                [in_ref[pl.ds((2 * p + half) * SLAB + z, GRID, stride=blocks * SLAB), :] for z in range(SLAB)], 0
            )
            for half in range(2)
        ]
        planes = backward(spectrum, base)
        for z in range(SLAB):
            out_ref[z] = out_ref[z] - both_ref[p - 1, z] * planes[z] if p else -occ_ref[z] * planes[z]


PARAMS = pltpu.CompilerParams(vmem_limit_bytes=40 * 2**20)
VM = pl.BlockSpec(memory_space=pltpu.VMEM)
SM = pl.BlockSpec(memory_space=pltpu.SMEM)


def call(kernel, shapes, ins, scalar=False, late=0, flops=1, scratch=()):
    many = isinstance(shapes, list)
    specs = [SM if scalar and k == 0 else VM for k in range(len(ins) - late)]
    return pl.pallas_call(
        kernel,
        out_shape=tuple(jax.ShapeDtypeStruct(s, f32) for s in shapes) if many else jax.ShapeDtypeStruct(shapes, f32),
        in_specs=specs + [pl.BlockSpec(memory_space=pl.ANY)] * late,
        out_specs=tuple(VM for _ in shapes) if many else VM,
        scratch_shapes=scratch,
        compiler_params=PARAMS,
        cost_estimate=pl.CostEstimate(flops=flops, bytes_accessed=1, transcendentals=0),
    )(*ins)


def exchange(value):
    return lax.all_to_all(value, "grid", split_axis=0, concat_axis=0, tiled=True)


def per_device(occupied, coefficients, slot_column, column_length):
    base, kernel = (jnp.asarray(table) for table in tables())
    grid_index = lax.axis_index("grid")
    index = grid_index.astype(jnp.int32).reshape(1)
    weight = lax.dynamic_index_in_dim(kernel, grid_index, 0, keepdims=False)
    step = (lax.axis_index("band") % LINE).astype(jnp.int32).reshape(1)
    occ = occupied.reshape(SLAB, N, N)
    half = SLAB // 2

    def place(x, z, y, core):
        return ((x % 4 * 2 + z % RING // 8) * LINE + y) * GRID + z % 8 * 2 + core

    def send(value, moves, route):
        pairs = []
        for x, z, core in itertools.product(range(4), range(RING), range(2)):
            side = z + 1 - 2 * core
            ends = {
                "stay": ((x, z), (x, z)),
                "aside": ((x, z), (x, side)),
                "across": ((x, z), (x + z // 8, z + 8)),
                "onward": ((x, side), (x + z // 8, z + 8)),
            }[route]
            for y, to in moves.items():
                pairs.append(tuple(place(*end, row, core) for end, row in zip(ends, (y, to))))
        return lax.ppermute(value, ("band", "grid"), pairs)

    near = send(occ[:half], {3: 0}, "across")
    far = send(occ[:half], {2: 0}, "across")
    spread = send(occ[half:], {3: 0, 2: 1}, "aside")
    back = send(spread, {0: 1, 1: 0}, "onward")
    one = send(occ, {0: 1, 1: 2, 2: 3}, "stay")
    two = send(one, {1: 2, 2: 3}, "stay")

    lines = call(
        lines_kernel,
        (N, CAP),
        (index, coefficients.reshape(K, CAP), column_length.reshape(-1, N), base, spread),
        scalar=True,
        late=1,
    )
    slab = exchange(lines.reshape(GRID, SLAB, CAP)).reshape(N, CAP)
    chosen = call(swap_kernel, (half, N, N), (step, near, back, far), scalar=True, late=1, flops=10**12)
    swap = send(chosen, {0: 1, 1: 0}, "stay")
    psi, sent = call(
        target_kernel,
        [(SLAB, N, N), (2 * N, N)],
        (slab, slot_column.reshape(-1, N), occ, base, chosen),
        late=1,
        scratch=(pltpu.VMEM((2 * N, GRID * CAP), bf16), pltpu.VMEM((OWN * K, GRID * CAP), bf16)),
    )
    sent, both = call(
        pair_kernel,
        [(6 * N, N), (2, SLAB, N, N)],
        (step, psi, one, two, near, far, back, swap, sent, base),
        scalar=True,
    )
    got = exchange(sent.reshape(GRID, 6 * SLAB, N))
    sent = call(pencil_kernel, (GRID, 6, SLAB, N), (got.reshape(GRID, 6, SLAB, N), weight, base))
    got = exchange(sent.reshape(GRID, 6 * SLAB, N))
    out = call(apply_kernel, (SLAB, N, N), (got.reshape(GRID * 6 * SLAB, N), occ, both, base))
    return out.reshape(1, SLAB, N, N)


def solution(mesh):
    placed = (P("band", "grid", None, None), P("band", None, "grid"), P(), P())
    return jax.shard_map(
        per_device,
        mesh=mesh,
        in_specs=placed,
        out_specs=P("band", "grid", None, None),
        check_vma=False,
    )
```

time: 207 us -> 134 us (0.65)
  the two profiles are of different devices: /device:TPU:25 before, /device:TPU:1 now
where the time goes in v2:
time: 134 us
  starting transfers between devices  56.2 us (42%)
  waiting for transfers between devices  34.4 us (26%)
  blocking collectives  27.6 us (21%)
  Pallas kernels  13.3 us (10%)
  local copies, waits for them, and re-layouts  1.96 us (1%)
    ppermute x7, starting transfers between devices, send(): return lax.ppermute(value, ('band', 'grid'), pairs)  30 us
    all_to_all x1, blocking collectives, exchange(): lax.all_to_all(value, 'grid', split_axis=0, concat_axis=0, tiled=True)  27.6 us
    all_to_all x2, waiting for transfers between devices, exchange(): lax.all_to_all(value, 'grid', split_axis=0, concat_axis=0, tiled=True)  26.3 us
    all_to_all x2, starting transfers between devices, exchange(): lax.all_to_all(value, 'grid', split_axis=0, concat_axis=0, tiled=True)  26.2 us
    pallas_call x6, Pallas kernels, call(): pl.pallas_call(kernel, out_shape=tuple((jax.ShapeDtypeStruct(s, f32) for...  13.3 us
    ppermute x7, waiting for transfers between devices, send(): return lax.ppermute(value, ('band', 'grid'), pairs)  8.14 us
  transfers between devices with their start and end apart: 9, of which 4 were waited for; matrix products, arithmetic and copies ran while one was open for 1% of the time, Pallas kernels for 5%

profile of v2, /device:TPU:1, one launch (start us, length us, event | category | flops | bytes accessed | tf_op | source)
XLA Modules:
  0.0 133.6 jit_solution(5636999432510897495)
XLA Ops:
  0.0 0.0 copy-start
  0.0 5.0 %collective-permute-start.4 = (f32[8,128,128]{2,1,0:T(8,128)}, f32[8,128,128]{2,1,0:T(8,128)}, u32[]{:S(2)}, u32[]{:S(2)}) collective-permute-start(f32[8,128,128]{2,1,0:T(8,128)} %bitcast.19), channel_id=1, source_target_pairs={{0,16},{16,32},{32,48},{1,17},{17,33},{33,49},{2,18},{18,34},{34,5... | collective-permute-start | bytes 1572872 | tf_op jit(solution)/shard_map/ppermute | solution.py:258
  5.0 0.0 copy-start.2
  5.0 1.1 slice_bitcast_fusion
  6.1 0.0 copy-start.4
  6.1 1.3 collective-permute-start
  7.4 1.3 collective-permute-start.1
  8.7 1.3 collective-permute-start.3
  10.0 5.3 %collective-permute-done.after = f32[4,128,128]{2,1,0:T(8,128)S(1)} collective-permute-done((f32[4,128,128]{2,1,0:T(8,128)S(1)}, f32[4,128,128]{2,1,0:T(8,128)S(1)}, u32[]{:S(2)}, u32[]{:S(2)}) %collective-permute-start) | collective-permute-done | bytes 262176 | tf_op jit(solution)/shard_map/ppermute | solution.py:258
  15.3 14.8 %collective-permute-start.2 = (f32[4,128,128]{2,1,0:T(8,128)S(1)}, f32[4,128,128]{2,1,0:T(8,128)S(1)}, u32[]{:S(2)}, u32[]{:S(2)}) collective-permute-start(f32[4,128,128]{2,1,0:T(8,128)S(1)} %collective-permute-done.after), channel_id=1, source_target_pairs={{2,80},{18,64},{79,81},{95,65},{4,82},{20,66},{1,83},{17,67},{6,84... | collective-permute-start | bytes 786440 | tf_op jit(solution)/shard_map/ppermute | solution.py:258
  30.1 0.0 copy-done
  30.1 0.0 copy-done.2
  30.1 0.0 copy-done.4
  30.1 0.9 shard_map.64
  31.0 16.7 %all-to-all-start = ((f32[16,8,384]{2,1,0:T(8,128)}), f32[16,8,384]{2,1,0:T(8,128)}, u32[]{:S(2)}, u32[]{:S(2)}) async-start(f32[16,8,384]{2,1,0:T(8,128)} %bitcast.5), calls=%async_computation | async-start | bytes 393216 | tf_op jit(solution)/shard_map/all_to_all | solution.py:231
  47.8 0.0 collective-permute-done.4.one
  47.8 1.5 %collective-permute-start.5 = (f32[8,128,128]{2,1,0:T(8,128)}, f32[8,128,128]{2,1,0:T(8,128)}, u32[]{:S(2)}, u32[]{:S(2)}) collective-permute-start(f32[8,128,128]{2,1,0:T(8,128)} %collective-permute-done.4.one), channel_id=1, source_target_pairs={{16,32},{32,48},{17,33},{33,49},{18,34},{34,50},{19,35},{35,51},{2... | collective-permute-start | bytes 1572872 | tf_op jit(solution)/shard_map/ppermute | solution.py:258
  49.3 0.0 collective-permute-done.1.near
  49.3 0.0 collective-permute-done.3.after.far
  49.3 2.8 %collective-permute-done.2.back = f32[4,128,128]{2,1,0:T(8,128)S(1)} collective-permute-done((f32[4,128,128]{2,1,0:T(8,128)S(1)}, f32[4,128,128]{2,1,0:T(8,128)S(1)}, u32[]{:S(2)}, u32[]{:S(2)}) %collective-permute-start.2) | collective-permute-done | bytes 262176 | tf_op jit(solution)/shard_map/ppermute | solution.py:258
  52.1 0.0 copy-start.1
  52.1 0.0 copy-start.3
  52.1 4.9 %collective-permute-start.6 = (f32[4,128,128]{2,1,0:T(8,128)S(1)}, f32[4,128,128]{2,1,0:T(8,128)S(1)}, u32[]{:S(2)}, u32[]{:S(2)}) collective-permute-start(f32[4,128,128]{2,1,0:T(8,128)S(1)} %shard_map.65.after), channel_id=1, source_target_pairs={{0,16},{16,0},{1,17},{17,1},{2,18},{18,2},{3,19},{19,3},{4,20},{20... | collective-permute-start | bytes 786440 | tf_op jit(solution)/shard_map/ppermute | solution.py:258
  57.0 5.5 %all-to-all-done = f32[16,8,384]{2,1,0:T(8,128)} async-done(((f32[16,8,384]{2,1,0:T(8,128)}), f32[16,8,384]{2,1,0:T(8,128)}, u32[]{:S(2)}, u32[]{:S(2)}) %all-to-all-start) | async-done | bytes 196640 | tf_op jit(solution)/shard_map/all_to_all | solution.py:231
  62.6 0.0 copy-done.1
  62.6 0.0 copy-done.3
  62.6 5.4 %shard_map.66 = (f32[8,128,128]{2,1,0:T(8,128)S(1)}, f32[256,128]{1,0:T(8,128)S(1)}) custom-call(f32[128,384]{1,0:T(8,128)} %bitcast.6.slab_ref, s32[48,128]{1,0:T(8,128)S(1)} %bitcast.26, f32[8,128,128]{2,1,0:T(8,128)S(1)} %bitcast.20, bf16[2,896,128]{2,1,0:T(8,128)(2,1)S(1)} %copy-done, f32[4,128,128]{2,1,0:T(8,128)S(1)} %shard_map.65.after), custom_call_target="tpu_custom_call" | custom-call | flops 1 | bytes 1 | tf_op jit(solution)/shard_map/pallas_call | solution.py:219
  68.0 0.0 collective-permute-done.6.swap
  68.0 0.0 collective-permute-done.5.two
  68.0 3.3 %shard_map.67 = (f32[768,128]{1,0:T(8,128)}, f32[2,8,128,128]{3,2,1,0:T(8,128)S(1)}) custom-call(s32[1]{0:T(128)} %bitcast.step_ref, f32[8,128,128]{2,1,0:T(8,128)S(1)} %get-tuple-element.9.psi_ref, f32[8,128,128]{2,1,0:T(8,128)} %collective-permute-done.4.one, f32[8,128,128]{2,1,0:T(8,128)} %collective-permute-done.5.two, ...), custom_call_target="tpu_custom_call" | custom-call | flops 1 | bytes 1 | tf_op jit(solution)/shard_map/pallas_call | solution.py:219
  71.3 9.4 %all-to-all-start.1 = ((f32[16,48,128]{2,1,0:T(8,128)}), f32[16,48,128]{2,1,0:T(8,128)S(1)}, u32[]{:S(2)}, u32[]{:S(2)}) async-start(f32[16,48,128]{2,1,0:T(8,128)} %bitcast.10), calls=%async_computation.1 | async-start | bytes 786432 | tf_op jit(solution)/shard_map/all_to_all | solution.py:231
  80.8 0.8 dynamic-slice_bitcast_fusion.weight
  81.6 20.8 %all-to-all-done.1 = f32[16,48,128]{2,1,0:T(8,128)S(1)} async-done(((f32[16,48,128]{2,1,0:T(8,128)}), f32[16,48,128]{2,1,0:T(8,128)S(1)}, u32[]{:S(2)}, u32[]{:S(2)}) %all-to-all-start.1) | async-done | bytes 393248 | tf_op jit(solution)/shard_map/all_to_all | solution.py:231
  102.4 1.4 %shard_map.68 = f32[16,6,8,128]{3,2,1,0:T(8,128)S(1)} custom-call(f32[16,6,8,128]{3,2,1,0:T(8,128)S(1)} %bitcast.22, f32[64,256]{1,0:T(8,128)S(1)} %dynamic-slice_bitcast_fusion.weight, bf16[2,896,128]{2,1,0:T(8,128)(2,1)S(1)} %copy-done), custom_call_target="tpu_custom_call" | custom-call | flops 1 | bytes 1 | tf_op jit(solution)/shard_map/pallas_call | solution.py:219
  103.8 27.6 %all_to_all.15 = f32[16,48,128]{2,1,0:T(8,128)S(1)} all-to-all(f32[16,48,128]{2,1,0:T(8,128)S(1)} %bitcast.23), channel_id=1, replica_groups=mesh['band'=32,'grid'=16] {'grid'}, dimensions={0} | all-to-all | bytes 786432 | tf_op jit(solution)/shard_map/all_to_all | solution.py:231
  131.4 2.3 %shard_map.69 = f32[8,128,128]{2,1,0:T(8,128)} custom-call(f32[768,128]{1,0:T(8,128)S(1)} %bitcast.24, f32[8,128,128]{2,1,0:T(8,128)S(1)} %bitcast.21, f32[2,8,128,128]{3,2,1,0:T(8,128)S(1)} %get-tuple-element.12.both_ref, bf16[2,896,128]{2,1,0:T(8,128)(2,1)S(1)} %copy-done), custom_call_target="tpu_custom_call" | custom-call | flops 1 | bytes 1 | tf_op jit(solution)/shard_map/pallas_call | solution.py:219
  (1 shorter events, 0.0 us)
Async XLA Ops:
  0.0 30.1 %copy-start = (bf16[2,896,128]{2,1,0:T(8,128)(2,1)S(1)}, bf16[2,896,128]{2,1,0:T(8,128)(2,1)}, u32[]{:S(2)}) copy-start(bf16[2,896,128]{2,1,0:T(8,128)(2,1)} %constant.31.clone.base) | copy-start | bytes 1376260
  0.0 47.8 %collective-permute-start.4 = (f32[8,128,128]{2,1,0:T(8,128)}, f32[8,128,128]{2,1,0:T(8,128)}, u32[]{:S(2)}, u32[]{:S(2)}) collective-permute-start(f32[8,128,128]{2,1,0:T(8,128)} %bitcast.19), channel_id=1, source_target_pairs={{0,16},{16,32},{32,48},{1,17},{17,33},{33,49},{2,18},{18,34},{34,5... | collective-permute-start | bytes 1572872 | tf_op jit(solution)/shard_map/ppermute | solution.py:258
  5.0 25.2 %copy-start.2 = (f32[1,64,384]{2,1,0:T(8,128)S(1)}, f32[1,64,384]{2,1,0:T(8,128)}, u32[]{:S(2)}) copy-start(f32[1,64,384]{2,1,0:T(8,128)} %param.7) | copy-start | bytes 294916
  6.1 24.1 %copy-start.4 = (s32[6144]{0:T(1024)S(1)}, s32[6144]{0:T(1024)}, u32[]{:S(2)}) copy-start(s32[6144]{0:T(1024)} %param.9) | copy-start | bytes 73732
  6.1 9.2 %collective-permute-start = (f32[4,128,128]{2,1,0:T(8,128)S(1)}, f32[4,128,128]{2,1,0:T(8,128)S(1)}, u32[]{:S(2)}, u32[]{:S(2)}) collective-permute-start(f32[4,128,128]{2,1,0:T(8,128)S(1)} %get-tuple-element.14), channel_id=1, source_target_pairs={{48,2},{32,18},{49,79},{33,95},{50,4},{34,20},{51,1},{35,17},{52,6... | collective-permute-start | bytes 786440 | tf_op jit(solution)/shard_map/ppermute | solution.py:258
  7.4 41.9 %collective-permute-start.1 = (f32[4,128,128]{2,1,0:T(8,128)S(1)}, f32[4,128,128]{2,1,0:T(8,128)S(1)}, u32[]{:S(2)}, u32[]{:S(2)}) collective-permute-start(f32[4,128,128]{2,1,0:T(8,128)S(1)} %get-tuple-element.13), channel_id=1, source_target_pairs={{48,64},{49,65},{50,66},{51,67},{52,68},{53,69},{54,70},{55,71},{5... | collective-permute-start | bytes 786440 | tf_op jit(solution)/shard_map/ppermute | solution.py:258
  8.7 40.6 %collective-permute-start.3 = (f32[4,128,128]{2,1,0:T(8,128)S(1)}, f32[4,128,128]{2,1,0:T(8,128)S(1)}, u32[]{:S(2)}, u32[]{:S(2)}) collective-permute-start(f32[4,128,128]{2,1,0:T(8,128)S(1)} %get-tuple-element.13), channel_id=1, source_target_pairs={{32,64},{33,65},{34,66},{35,67},{36,68},{37,69},{38,70},{39,71},{4... | collective-permute-start | bytes 786440 | tf_op jit(solution)/shard_map/ppermute | solution.py:258
  15.3 36.8 %collective-permute-start.2 = (f32[4,128,128]{2,1,0:T(8,128)S(1)}, f32[4,128,128]{2,1,0:T(8,128)S(1)}, u32[]{:S(2)}, u32[]{:S(2)}) collective-permute-start(f32[4,128,128]{2,1,0:T(8,128)S(1)} %collective-permute-done.after), channel_id=1, source_target_pairs={{2,80},{18,64},{79,81},{95,65},{4,82},{20,66},{1,83},{17,67},{6,84... | collective-permute-start | bytes 786440 | tf_op jit(solution)/shard_map/ppermute | solution.py:258
  31.0 31.5 %all-to-all-start = ((f32[16,8,384]{2,1,0:T(8,128)}), f32[16,8,384]{2,1,0:T(8,128)}, u32[]{:S(2)}, u32[]{:S(2)}) async-start(f32[16,8,384]{2,1,0:T(8,128)} %bitcast.5), calls=%async_computation | async-start | bytes 393216 | tf_op jit(solution)/shard_map/all_to_all | solution.py:231
  47.8 20.2 %collective-permute-start.5 = (f32[8,128,128]{2,1,0:T(8,128)}, f32[8,128,128]{2,1,0:T(8,128)}, u32[]{:S(2)}, u32[]{:S(2)}) collective-permute-start(f32[8,128,128]{2,1,0:T(8,128)} %collective-permute-done.4.one), channel_id=1, source_target_pairs={{16,32},{32,48},{17,33},{33,49},{18,34},{34,50},{19,35},{35,51},{2... | collective-permute-start | bytes 1572872 | tf_op jit(solution)/shard_map/ppermute | solution.py:258
  52.1 10.5 %copy-start.1 = (f32[1,8,128,128]{3,2,1,0:T(8,128)S(1)}, f32[1,8,128,128]{3,2,1,0:T(8,128)}, u32[]{:S(2)}) copy-start(f32[1,8,128,128]{3,2,1,0:T(8,128)} %param.6) | copy-start | bytes 1572868
  52.1 10.5 %copy-start.3 = (s32[6144]{0:T(1024)S(1)}, s32[6144]{0:T(1024)}, u32[]{:S(2)}) copy-start(s32[6144]{0:T(1024)} %param.8) | copy-start | bytes 73732
  52.1 15.9 %collective-permute-start.6 = (f32[4,128,128]{2,1,0:T(8,128)S(1)}, f32[4,128,128]{2,1,0:T(8,128)S(1)}, u32[]{:S(2)}, u32[]{:S(2)}) collective-permute-start(f32[4,128,128]{2,1,0:T(8,128)S(1)} %shard_map.65.after), channel_id=1, source_target_pairs={{0,16},{16,0},{1,17},{17,1},{2,18},{18,2},{3,19},{19,3},{4,20},{20... | collective-permute-start | bytes 786440 | tf_op jit(solution)/shard_map/ppermute | solution.py:258
  71.3 31.0 %all-to-all-start.1 = ((f32[16,48,128]{2,1,0:T(8,128)}), f32[16,48,128]{2,1,0:T(8,128)S(1)}, u32[]{:S(2)}, u32[]{:S(2)}) async-start(f32[16,48,128]{2,1,0:T(8,128)} %bitcast.10), calls=%async_computation.1 | async-start | bytes 786432 | tf_op jit(solution)/shard_map/all_to_all | solution.py:231

commit v3 on v2

--- a/solution.py
+++ b/solution.py
@@ -21,9 +21,8 @@
 LINE = 4
 RING = 16
 f32, bf16 = jnp.float32, jnp.bfloat16
-SHAPES = dict(
-    pack=(N, K), twice=(N, N), rows=(K, N), cols=(N, K), diag=(2 * N, N), depth=(K, N), depth_t=(N, K)
-)
+LEFTS = dict(pack=(N, K), rows=(K, N), cols=(N, K), depth=(K, N), depth_t=(N, K))
+RIGHTS = dict(twice=(N, N), diag=(N, 2 * N))
 
 
 def cas(freq, coord):
@@ -32,11 +31,17 @@
     return (np.cos(angle) + np.sin(angle)) / math.sqrt(N)
 
 
-def halves(table):
+def terms(table, axis):
     table = np.asarray(table, np.float32)
     high = table.astype(ml_dtypes.bfloat16)
     low = (table - high.astype(np.float32)).astype(ml_dtypes.bfloat16)
-    return np.stack([high, low])
+    return np.concatenate([high, high, low], axis)
+
+
+def stack(named, axis):
+    parts = [terms(table, axis) for table in named.values()]
+    width = max(p.shape[1] for p in parts)
+    return np.concatenate([np.pad(p, ((0, 0), (0, width - p.shape[1]))) for p in parts])
 
 
 def tables():
@@ -55,26 +60,37 @@
     kernel = np.where(total >= (N // 4) ** 2, 0.0, kernel)
     kernel = kernel.reshape(K, GRID, OWN * K).transpose(1, 0, 2)
     zero = np.zeros((K, N))
-    named = dict(
+    lefts = dict(
         pack=cas(packed_freq, points).T,
-        twice=np.concatenate([basis.T, basis.T], 1),
         rows=basis[order],
         cols=basis[order].T,
-        diag=np.concatenate([np.block([[basis], [zero]]), np.block([[zero], [basis]])]),
         depth=basis,
         depth_t=basis.T,
     )
-    assert {name: table.shape for name, table in named.items()} == SHAPES
-    base = np.concatenate([np.pad(t, ((0, 0), (0, N - t.shape[1]))) for t in named.values()])
-    return halves(base), kernel.astype(np.float32)
-
-
-def view(base, name):
+    rights = dict(
+        twice=np.concatenate([basis.T, basis.T], 1),
+        diag=np.block([[basis, zero], [zero, basis]]),
+    )
+    for named, shapes in ((lefts, LEFTS), (rights, RIGHTS)):
+        assert {name: table.shape for name, table in named.items()} == shapes
+    return stack(lefts, 1), stack(rights, 0), kernel.astype(np.float32)
+
+
+def left_table(base, name):
     start = 0
-    for other, (height, width) in SHAPES.items():
+    for other, (height, width) in LEFTS.items():
         if other == name:
-            return [base[h, start : start + height, :width] for h in range(2)]
+            return base[start : start + height, : 3 * width]
         start += height
+    raise KeyError(name)
+
+
+def right_table(base, name):
+    start = 0
+    for other, (height, width) in RIGHTS.items():
+        if other == name:
+            return base[start : start + 3 * height, :width]
+        start += 3 * height
     raise KeyError(name)
 
 
@@ -89,39 +105,41 @@
 
 def right(value, table):
     high, low = split(value)
-    return mul(high, table[0]) + mul(low, table[0]) + mul(high, table[1])
+    return mul(jnp.concatenate([high, low, high], 1), table)
 
 
 def left(table, value):
     high, low = split(value)
-    return mul(table[0], high) + mul(table[0], low) + mul(table[1], high)
-
-
-def forward(pair, store, base):
-    twice, rows = view(base, "twice"), view(base, "rows")
-    first = right(pair.reshape(SLAB * N, N), twice)
+    return mul(table, jnp.concatenate([high, low, high], 0))
+
+
+def forward(pair, store, lefts, rights):
+    first = right(pair.reshape(SLAB * N, N), right_table(rights, "twice"))
+    rows = left_table(lefts, "rows")
     lane = lax.broadcasted_iota(jnp.int32, (GRID, N), 1) < K
-    for z in range(SLAB):
-        both = left(rows, first[z * N : (z + 1) * N])
-        part = [both[low * GRID : (low + 1) * GRID] for low in range(OWN)]
-        store(z, 0, jnp.where(lane, part[0], part[1]))
-        store(z, 1, jnp.where(lane, part[2], part[3]))
-
-
-def backward(spectrum, base):
-    diag, cols = view(base, "diag"), view(base, "cols")
-    part = []
-    for half in range(2):
-        part += [right(spectrum[half], [h[low * N : (low + 1) * N] for h in diag]) for low in range(2)]
+    for z in range(0, SLAB, 2):
+        both = left(rows, jnp.concatenate([first[z * N : (z + 1) * N], first[(z + 1) * N : (z + 2) * N]], 1))
+        for k in range(2):
+            part = [both[low * GRID : (low + 1) * GRID, k * N : (k + 1) * N] for low in range(OWN)]
+            store(z + k, 0, jnp.where(lane, part[0], part[1]))
+            store(z + k, 1, jnp.where(lane, part[2], part[3]))
+
+
+def backward(spectrum, lefts, rights):
+    diag = right_table(rights, "diag")
+    cols = left_table(lefts, "cols")
+    lines = [right(half, diag) for half in spectrum]
+    part = [line[:, k * N : (k + 1) * N] for line in lines for k in range(2)]
     out = []
-    for z in range(SLAB):
-        stacked = jnp.concatenate([p[z * GRID : (z + 1) * GRID] for p in part], 0)
-        out.append(left(cols, stacked))
+    for z in range(0, SLAB, 2):
+        stacked = [jnp.concatenate([p[w * GRID : (w + 1) * GRID] for p in part], 0) for w in (z, z + 1)]
+        planes = left(cols, jnp.concatenate(stacked, 1))
+        out += [planes[:, :N], planes[:, N:]]
     return out
 
 
-def lines_kernel(index_ref, coef_ref, length_ref, base, after, out_ref):
-    pack = view(base, "pack")
+def lines_kernel(index_ref, coef_ref, length_ref, lefts, out_ref):
+    pack = left_table(lefts, "pack")
     start = index_ref[0] * (CAP // N)
     entry = lax.broadcasted_iota(jnp.int32, (K, N), 0)
     for j in range(CAP // N):
@@ -130,7 +148,7 @@
         out_ref[:, j * N : (j + 1) * N] = left(pack, live)
 
 
-def target_kernel(slab_ref, slot_ref, occ_ref, base, after, psi_ref, out_ref, values, picks):
+def target_kernel(slab_ref, slot_ref, occ_ref, lefts, rights, psi_ref, out_ref, values, picks):
     owner = lax.broadcasted_iota(jnp.int32, (GRID, N), 0)
     place = lax.broadcasted_iota(jnp.int32, (OWN * K, N), 0)
     for chunk in range(GRID * CAP // N):
@@ -151,21 +169,25 @@
                 values[row : row + GRID, lanes] = jnp.where(hit, part[z : z + 1], 0.0).astype(bf16)
     both = lax.dot_general(values[...], picks[...], (((1,), (1,)), ((), ())), preferred_element_type=f32)
     spectrum = both[:N] + both[N:]
-    planes = backward([spectrum[:, :N], spectrum[:, N:]], base)
+    planes = backward([spectrum[:, :N], spectrum[:, N:]], lefts, rights)
     for z in range(SLAB):
         psi_ref[z] = planes[z]
 
     def store(z, half, value):
         out_ref[pl.ds(half * SLAB + z, GRID, stride=2 * SLAB), :] = value
 
-    forward(occ_ref[...] * psi_ref[...], store, base)
-
-
-def swap_kernel(step_ref, near, back, after, out_ref):
+    forward(occ_ref[...] * psi_ref[...], store, lefts, rights)
+
+
+def hold_kernel(value, after, out_ref):
+    out_ref[...] = value[...]
+
+
+def swap_kernel(step_ref, near, back, after, also, out_ref):
     out_ref[...] = jnp.where(step_ref[0] == 0, near[...], back[...])
 
 
-def pair_kernel(step_ref, psi_ref, one, two, near, far, back, swap, own_ref, base, out_ref, occ_ref):
+def pair_kernel(step_ref, psi_ref, one, two, near, far, back, swap, own_ref, lefts, rights, out_ref, occ_ref):
     half = SLAB // 2
     first, second = step_ref[0] == 0, step_ref[0] == 1
     occ_ref[0, :half] = jnp.where(first, near[...], one[:half])
@@ -182,18 +204,19 @@
         def store(z, half, value):
             out_ref[pl.ds((2 + 2 * p + half) * SLAB + z, GRID, stride=blocks * SLAB), :] = value
 
-        forward(occ_ref[p] * psi_ref[...], store, base)
-
-
-def pencil_kernel(in_ref, weight, base, out_ref):
-    depth, depth_t = view(base, "depth"), view(base, "depth_t")
-    for k in range(in_ref.shape[1]):
-        half = k % 2
-        scaled = left(depth, in_ref[:, k].reshape(N, N)) * weight[:, half * N : (half + 1) * N]
-        out_ref[:, k] = left(depth_t, scaled).reshape(GRID, SLAB, N)
-
-
-def apply_kernel(in_ref, occ_ref, both_ref, base, out_ref):
+        forward(occ_ref[p] * psi_ref[...], store, lefts, rights)
+
+
+def pencil_kernel(in_ref, weight, lefts, out_ref):
+    depth, depth_t = left_table(lefts, "depth"), left_table(lefts, "depth_t")
+    for p in range(in_ref.shape[1] // 2):
+        lines = jnp.concatenate([in_ref[:, 2 * p + half].reshape(N, N) for half in range(2)], 1)
+        lines = left(depth_t, left(depth, lines) * weight[...])
+        for half in range(2):
+            out_ref[:, 2 * p + half] = lines[:, half * N : (half + 1) * N].reshape(GRID, SLAB, N)
+
+
+def apply_kernel(in_ref, occ_ref, both_ref, lefts, rights, out_ref):
     count = 1 + both_ref.shape[0]
     blocks = in_ref.shape[0] // (GRID * SLAB)
     for p in range(count):
@@ -203,12 +226,12 @@
             )
             for half in range(2)
         ]
-        planes = backward(spectrum, base)
+        planes = backward(spectrum, lefts, rights)
         for z in range(SLAB):
             out_ref[z] = out_ref[z] - both_ref[p - 1, z] * planes[z] if p else -occ_ref[z] * planes[z]
 
 
-PARAMS = pltpu.CompilerParams(vmem_limit_bytes=40 * 2**20)
+PARAMS = pltpu.CompilerParams(vmem_limit_bytes=50 * 2**20)
 VM = pl.BlockSpec(memory_space=pltpu.VMEM)
 SM = pl.BlockSpec(memory_space=pltpu.SMEM)
 
@@ -232,7 +255,7 @@
 
 
 def per_device(occupied, coefficients, slot_column, column_length):
-    base, kernel = (jnp.asarray(table) for table in tables())
+    lefts, rights, kernel = (jnp.asarray(table) for table in tables())
     grid_index = lax.axis_index("grid")
     index = grid_index.astype(jnp.int32).reshape(1)
     weight = lax.dynamic_index_in_dim(kernel, grid_index, 0, keepdims=False)
@@ -260,37 +283,36 @@
     near = send(occ[:half], {3: 0}, "across")
     far = send(occ[:half], {2: 0}, "across")
     spread = send(occ[half:], {3: 0, 2: 1}, "aside")
-    back = send(spread, {0: 1, 1: 0}, "onward")
-    one = send(occ, {0: 1, 1: 2, 2: 3}, "stay")
-    two = send(one, {1: 2, 2: 3}, "stay")
 
     lines = call(
         lines_kernel,
         (N, CAP),
-        (index, coefficients.reshape(K, CAP), column_length.reshape(-1, N), base, spread),
+        (index, coefficients.reshape(K, CAP), column_length.reshape(-1, N), lefts),
         scalar=True,
-        late=1,
-    )
+    )
+    spread = call(hold_kernel, spread.shape, (spread, lines), late=1, flops=10**12)
+    back = send(spread, {0: 1, 1: 0}, "onward")
     slab = exchange(lines.reshape(GRID, SLAB, CAP)).reshape(N, CAP)
-    chosen = call(swap_kernel, (half, N, N), (step, near, back, far), scalar=True, late=1, flops=10**12)
-    swap = send(chosen, {0: 1, 1: 0}, "stay")
+    one = send(occ, {0: 1, 1: 2, 2: 3}, "stay")
+    two = send(occ, {0: 2, 1: 3}, "stay")
     psi, sent = call(
         target_kernel,
         [(SLAB, N, N), (2 * N, N)],
-        (slab, slot_column.reshape(-1, N), occ, base, chosen),
-        late=1,
+        (slab, slot_column.reshape(-1, N), occ, lefts, rights),
         scratch=(pltpu.VMEM((2 * N, GRID * CAP), bf16), pltpu.VMEM((OWN * K, GRID * CAP), bf16)),
     )
+    chosen = call(swap_kernel, (half, N, N), (step, near, back, far, psi), scalar=True, late=2)
+    swap = send(chosen, {0: 1, 1: 0}, "stay")
     sent, both = call(
         pair_kernel,
         [(6 * N, N), (2, SLAB, N, N)],
-        (step, psi, one, two, near, far, back, swap, sent, base),
+        (step, psi, one, two, near, far, back, swap, sent, lefts, rights),
         scalar=True,
     )
     got = exchange(sent.reshape(GRID, 6 * SLAB, N))
-    sent = call(pencil_kernel, (GRID, 6, SLAB, N), (got.reshape(GRID, 6, SLAB, N), weight, base))
+    sent = call(pencil_kernel, (GRID, 6, SLAB, N), (got.reshape(GRID, 6, SLAB, N), weight, lefts))
     got = exchange(sent.reshape(GRID, 6 * SLAB, N))
-    out = call(apply_kernel, (SLAB, N, N), (got.reshape(GRID * 6 * SLAB, N), occ, both, base))
+    out = call(apply_kernel, (SLAB, N, N), (got.reshape(GRID * 6 * SLAB, N), occ, both, lefts, rights))
     return out.reshape(1, SLAB, N, N)
 
 

time: 134 us -> 131 us (0.978)
  starting transfers between devices: 56.2 us -> 49.4 us
  waiting for transfers between devices: 34.4 us -> 38.4 us
    all_to_all x2, waiting for transfers between devices: 26.3 us -> 32.2 us  [exchange(): lax.all_to_all(value, 'grid', split_axis=0, concat_axis=0, tiled=True)]
    ppermute x7, starting transfers between devices: 30 us -> 24.4 us  [send(): return lax.ppermute(value, ('band', 'grid'), pairs)]
    ppermute x7, waiting for transfers between devices: 8.14 us -> 6.16 us  [send(): return lax.ppermute(value, ('band', 'grid'), pairs)]
    pallas_call x6 -> x7, Pallas kernels: 13.3 us -> 12 us  [call(): pl.pallas_call(kernel, out_shape=tuple((jax.ShapeDtypeStruct(s, f32) for...]
  transfers between devices with their start and end apart: 9 -> 9, of which waited for: 4 -> 3; matrix products, arithmetic and copies ran while one was open for 1% -> 1% of each run, Pallas kernels for 5% -> 5%
where the time goes in v3:
time: 131 us; the launch traced here: 130 us
  starting transfers between devices  49.4 us (38%)
  waiting for transfers between devices  38.4 us (29%)
  blocking collectives  27.6 us (21%)
  Pallas kernels  12 us (9%)
  local copies, waits for them, and re-layouts  2.7 us (2%)
    all_to_all x2, waiting for transfers between devices, exchange(): lax.all_to_all(value, 'grid', split_axis=0, concat_axis=0, tiled=True)  32.2 us
    all_to_all x1, blocking collectives, exchange(): lax.all_to_all(value, 'grid', split_axis=0, concat_axis=0, tiled=True)  27.6 us
    all_to_all x2, starting transfers between devices, exchange(): lax.all_to_all(value, 'grid', split_axis=0, concat_axis=0, tiled=True)  25 us
    ppermute x7, starting transfers between devices, send(): return lax.ppermute(value, ('band', 'grid'), pairs)  24.4 us
    pallas_call x7, Pallas kernels, call(): pl.pallas_call(kernel, out_shape=tuple((jax.ShapeDtypeStruct(s, f32) for...  12 us
    ppermute x7, waiting for transfers between devices, send(): return lax.ppermute(value, ('band', 'grid'), pairs)  6.16 us
  transfers between devices with their start and end apart: 9, of which 3 were waited for; matrix products, arithmetic and copies ran while one was open for 1% of the time, Pallas kernels for 5%

profile of v3, /device:TPU:1, one launch (start us, length us, event | category | flops | bytes accessed | tf_op | source)
XLA Modules:
  0.0 130.3 jit_solution(11393453624048900535)
XLA Ops:
  0.0 0.0 copy-start
  0.0 0.0 copy-start.4
  0.0 0.0 copy-start.5
  0.0 1.8 %slice_bitcast_fusion = (f32[4,128,128]{2,1,0:T(8,128)S(1)}, f32[4,128,128]{2,1,0:T(8,128)}) fusion(f32[1,8,128,128]{3,2,1,0:T(8,128)} %param.7), kind=kLoop, calls=%fused_computation | loop fusion | bytes 1048576 | tf_op jit(solution)/shard_map/slice | solution.py:285
  1.8 1.3 collective-permute-start.4
  3.1 1.3 collective-permute-start.2
  4.4 1.3 collective-permute-start.3
  5.7 0.0 copy-done
  5.7 0.0 copy-done.4
  5.7 0.0 copy-done.5
  5.8 0.9 shard_map.73.after
  6.6 14.0 %all-to-all-start = ((f32[16,8,384]{2,1,0:T(8,128)}), f32[16,8,384]{2,1,0:T(8,128)}, u32[]{:S(2)}, u32[]{:S(2)}) async-start(f32[16,8,384]{2,1,0:T(8,128)} %bitcast.4), calls=%async_computation | async-start | bytes 393216 | tf_op jit(solution)/shard_map/all_to_all | solution.py:254
  20.7 0.0 collective-permute-done.4.value
  20.7 0.0 copy-start.1
  20.7 0.0 copy-start.2
  20.7 0.0 copy-start.6
  20.8 9.4 %collective-permute-start.5 = (f32[4,128,128]{2,1,0:T(8,128)S(1)}, f32[4,128,128]{2,1,0:T(8,128)S(1)}, u32[]{:S(2)}, u32[]{:S(2)}) collective-permute-start(f32[4,128,128]{2,1,0:T(8,128)S(1)} %shard_map.75), channel_id=1, source_target_pairs={{2,80},{18,64},{79,81},{95,65},{4,82},{20,66},{1,83},{17,67},{6,84... | collective-permute-start | bytes 786440 | tf_op jit(solution)/shard_map/ppermute | solution.py:281
  30.2 0.0 copy-done.1
  30.2 2.0 %collective-permute-start = (f32[8,128,128]{2,1,0:T(8,128)S(1)}, f32[8,128,128]{2,1,0:T(8,128)S(1)}, u32[]{:S(2)}, u32[]{:S(2)}) collective-permute-start(f32[8,128,128]{2,1,0:T(8,128)S(1)} %bitcast.19), channel_id=1, source_target_pairs={{0,16},{16,32},{32,48},{1,17},{17,33},{33,49},{2,18},{18,34},{34,5... | collective-permute-start | bytes 1572872 | tf_op jit(solution)/shard_map/ppermute | solution.py:281
  32.2 4.7 %collective-permute-start.1 = (f32[8,128,128]{2,1,0:T(8,128)S(1)}, f32[8,128,128]{2,1,0:T(8,128)S(1)}, u32[]{:S(2)}, u32[]{:S(2)}) collective-permute-start(f32[8,128,128]{2,1,0:T(8,128)S(1)} %bitcast.20), channel_id=1, source_target_pairs={{0,32},{16,48},{1,33},{17,49},{2,34},{18,50},{3,35},{19,51},{4,36}... | collective-permute-start | bytes 1572872 | tf_op jit(solution)/shard_map/ppermute | solution.py:281
  36.9 11.5 %all-to-all-done = f32[16,8,384]{2,1,0:T(8,128)} async-done(((f32[16,8,384]{2,1,0:T(8,128)}), f32[16,8,384]{2,1,0:T(8,128)}, u32[]{:S(2)}, u32[]{:S(2)}) %all-to-all-start) | async-done | bytes 196640 | tf_op jit(solution)/shard_map/all_to_all | solution.py:254
  48.4 0.0 copy-done.2
  48.4 0.0 copy-done.6
  48.4 4.8 %shard_map.74 = (f32[8,128,128]{2,1,0:T(8,128)S(1)}, f32[256,128]{1,0:T(8,128)S(1)}) custom-call(f32[128,384]{1,0:T(8,128)} %bitcast.5.slab_ref, s32[48,128]{1,0:T(8,128)S(1)} %bitcast.28, f32[8,128,128]{2,1,0:T(8,128)S(1)} %bitcast.21, bf16[512,384]{1,0:T(8,128)(2,1)S(1)} %copy-done, bf16[768,256]{1,0:T(8,128)(2,1)S(1)} %copy-done.2), custom_call_target="tpu_custom_call" | custom-call | flops 1 | bytes 1 | tf_op jit(solution)/shard_map/pallas_call | solution.py:242
  53.1 0.0 collective-permute-done.2.near
  53.1 0.0 collective-permute-done.3.after.far
  53.2 0.0 collective-permute-done.5.back
  53.2 1.0 shard_map.76
  54.1 4.5 %collective-permute-start.6 = (f32[4,128,128]{2,1,0:T(8,128)S(1)}, f32[4,128,128]{2,1,0:T(8,128)S(1)}, u32[]{:S(2)}, u32[]{:S(2)}) collective-permute-start(f32[4,128,128]{2,1,0:T(8,128)S(1)} %shard_map.76), channel_id=1, source_target_pairs={{0,16},{16,0},{1,17},{17,1},{2,18},{18,2},{3,19},{19,3},{4,20},{20... | collective-permute-start | bytes 786440 | tf_op jit(solution)/shard_map/ppermute | solution.py:281
  58.6 0.0 collective-permute-done.one
  58.6 0.0 collective-permute-done.1.two
  58.6 6.1 %collective-permute-done.6.swap = f32[4,128,128]{2,1,0:T(8,128)S(1)} collective-permute-done((f32[4,128,128]{2,1,0:T(8,128)S(1)}, f32[4,128,128]{2,1,0:T(8,128)S(1)}, u32[]{:S(2)}, u32[]{:S(2)}) %collective-permute-start.6) | collective-permute-done | bytes 262176 | tf_op jit(solution)/shard_map/ppermute | solution.py:281
  64.8 2.8 %shard_map.77 = (f32[768,128]{1,0:T(8,128)}, f32[2,8,128,128]{3,2,1,0:T(8,128)}) custom-call(s32[1]{0:T(128)} %bitcast.step_ref, f32[8,128,128]{2,1,0:T(8,128)S(1)} %get-tuple-element.9.also.psi_ref, f32[8,128,128]{2,1,0:T(8,128)S(1)} %collective-permute-done.one, f32[8,128,128]{2,1,0:T(8,128)S(1)} %collective-permute-done.1.two, ...), custom_call_target="tpu_custom_call" | custom-call | flops 1 | bytes 1 | tf_op jit(solution)/shard_map/pallas_call | solution.py:242
  67.6 11.0 %all-to-all-start.1 = ((f32[16,48,128]{2,1,0:T(8,128)}), f32[16,48,128]{2,1,0:T(8,128)S(1)}, u32[]{:S(2)}, u32[]{:S(2)}) async-start(f32[16,48,128]{2,1,0:T(8,128)} %bitcast.10), calls=%async_computation.1 | async-start | bytes 786432 | tf_op jit(solution)/shard_map/all_to_all | solution.py:254
  78.5 0.8 dynamic-slice_bitcast_fusion.weight
  79.4 0.0 copy-start.3
  79.4 20.8 %all-to-all-done.1 = f32[16,48,128]{2,1,0:T(8,128)S(1)} async-done(((f32[16,48,128]{2,1,0:T(8,128)}), f32[16,48,128]{2,1,0:T(8,128)S(1)}, u32[]{:S(2)}, u32[]{:S(2)}) %all-to-all-start.1) | async-done | bytes 393248 | tf_op jit(solution)/shard_map/all_to_all | solution.py:254
  100.1 0.7 shard_map.78
  100.9 27.6 %all_to_all.15 = f32[16,48,128]{2,1,0:T(8,128)S(1)} all-to-all(f32[16,48,128]{2,1,0:T(8,128)S(1)} %bitcast.25), channel_id=1, replica_groups=mesh['band'=32,'grid'=16] {'grid'}, dimensions={0} | all-to-all | bytes 786432 | tf_op jit(solution)/shard_map/all_to_all | solution.py:254
  128.5 0.0 copy-done.3
  128.5 1.8 %shard_map.79 = f32[8,128,128]{2,1,0:T(8,128)} custom-call(f32[768,128]{1,0:T(8,128)S(1)} %bitcast.24, f32[8,128,128]{2,1,0:T(8,128)S(1)} %bitcast.22, f32[2,8,128,128]{3,2,1,0:T(8,128)S(1)} %copy-done.3, bf16[512,384]{1,0:T(8,128)(2,1)S(1)} %copy-done, bf16[768,256]{1,0:T(8,128)(2,1)S(1)} %copy-done.2), custom_call_target="tpu_custom_call" | custom-call | flops 1 | bytes 1 | tf_op jit(solution)/shard_map/pallas_call | solution.py:242
  (1 shorter events, 0.0 us)
Async XLA Ops:
  0.0 5.7 %copy-start = (bf16[512,384]{1,0:T(8,128)(2,1)S(1)}, bf16[512,384]{1,0:T(8,128)(2,1)}, u32[]{:S(2)}) copy-start(bf16[512,384]{1,0:T(8,128)(2,1)} %constant.33.clone.lefts) | copy-start | bytes 1179652
  0.0 5.7 %copy-start.4 = (f32[1,64,384]{2,1,0:T(8,128)S(1)}, f32[1,64,384]{2,1,0:T(8,128)}, u32[]{:S(2)}) copy-start(f32[1,64,384]{2,1,0:T(8,128)} %param.8) | copy-start | bytes 294916
  0.0 5.7 %copy-start.5 = (s32[6144]{0:T(1024)S(1)}, s32[6144]{0:T(1024)}, u32[]{:S(2)}) copy-start(s32[6144]{0:T(1024)} %param.10) | copy-start | bytes 73732
  1.8 18.9 %collective-permute-start.4 = (f32[4,128,128]{2,1,0:T(8,128)S(1)}, f32[4,128,128]{2,1,0:T(8,128)S(1)}, u32[]{:S(2)}, u32[]{:S(2)}) collective-permute-start(f32[4,128,128]{2,1,0:T(8,128)S(1)} %get-tuple-element.13), channel_id=1, source_target_pairs={{48,2},{32,18},{49,79},{33,95},{50,4},{34,20},{51,1},{35,17},{52,6... | collective-permute-start | bytes 786440 | tf_op jit(solution)/shard_map/ppermute | solution.py:281
  3.1 50.0 %collective-permute-start.2 = (f32[4,128,128]{2,1,0:T(8,128)}, f32[4,128,128]{2,1,0:T(8,128)}, u32[]{:S(2)}, u32[]{:S(2)}) collective-permute-start(f32[4,128,128]{2,1,0:T(8,128)} %get-tuple-element.14), channel_id=1, source_target_pairs={{48,64},{49,65},{50,66},{51,67},{52,68},{53,69},{54,70},{55,71},{5... | collective-permute-start | bytes 786440 | tf_op jit(solution)/shard_map/ppermute | solution.py:281
  4.4 48.7 %collective-permute-start.3 = (f32[4,128,128]{2,1,0:T(8,128)}, f32[4,128,128]{2,1,0:T(8,128)}, u32[]{:S(2)}, u32[]{:S(2)}) collective-permute-start(f32[4,128,128]{2,1,0:T(8,128)} %get-tuple-element.14), channel_id=1, source_target_pairs={{32,64},{33,65},{34,66},{35,67},{36,68},{37,69},{38,70},{39,71},{4... | collective-permute-start | bytes 786440 | tf_op jit(solution)/shard_map/ppermute | solution.py:281
  6.6 41.7 %all-to-all-start = ((f32[16,8,384]{2,1,0:T(8,128)}), f32[16,8,384]{2,1,0:T(8,128)}, u32[]{:S(2)}, u32[]{:S(2)}) async-start(f32[16,8,384]{2,1,0:T(8,128)} %bitcast.4), calls=%async_computation | async-start | bytes 393216 | tf_op jit(solution)/shard_map/all_to_all | solution.py:254
  20.7 9.5 %copy-start.1 = (f32[1,8,128,128]{3,2,1,0:T(8,128)S(1)}, f32[1,8,128,128]{3,2,1,0:T(8,128)}, u32[]{:S(2)}) copy-start(f32[1,8,128,128]{3,2,1,0:T(8,128)} %param.7) | copy-start | bytes 1572868
  20.7 27.6 %copy-start.2 = (bf16[768,256]{1,0:T(8,128)(2,1)S(1)}, bf16[768,256]{1,0:T(8,128)(2,1)}, u32[]{:S(2)}) copy-start(bf16[768,256]{1,0:T(8,128)(2,1)} %constant.34.clone.rights) | copy-start | bytes 1179652
  20.7 27.6 %copy-start.6 = (s32[6144]{0:T(1024)S(1)}, s32[6144]{0:T(1024)}, u32[]{:S(2)}) copy-start(s32[6144]{0:T(1024)} %param.9) | copy-start | bytes 73732
  20.8 32.4 %collective-permute-start.5 = (f32[4,128,128]{2,1,0:T(8,128)S(1)}, f32[4,128,128]{2,1,0:T(8,128)S(1)}, u32[]{:S(2)}, u32[]{:S(2)}) collective-permute-start(f32[4,128,128]{2,1,0:T(8,128)S(1)} %shard_map.75), channel_id=1, source_target_pairs={{2,80},{18,64},{79,81},{95,65},{4,82},{20,66},{1,83},{17,67},{6,84... | collective-permute-start | bytes 786440 | tf_op jit(solution)/shard_map/ppermute | solution.py:281
  30.2 28.4 %collective-permute-start = (f32[8,128,128]{2,1,0:T(8,128)S(1)}, f32[8,128,128]{2,1,0:T(8,128)S(1)}, u32[]{:S(2)}, u32[]{:S(2)}) collective-permute-start(f32[8,128,128]{2,1,0:T(8,128)S(1)} %bitcast.19), channel_id=1, source_target_pairs={{0,16},{16,32},{32,48},{1,17},{17,33},{33,49},{2,18},{18,34},{34,5... | collective-permute-start | bytes 1572872 | tf_op jit(solution)/shard_map/ppermute | solution.py:281
  32.2 26.4 %collective-permute-start.1 = (f32[8,128,128]{2,1,0:T(8,128)S(1)}, f32[8,128,128]{2,1,0:T(8,128)S(1)}, u32[]{:S(2)}, u32[]{:S(2)}) collective-permute-start(f32[8,128,128]{2,1,0:T(8,128)S(1)} %bitcast.20), channel_id=1, source_target_pairs={{0,32},{16,48},{1,33},{17,49},{2,34},{18,50},{3,35},{19,51},{4,36}... | collective-permute-start | bytes 1572872 | tf_op jit(solution)/shard_map/ppermute | solution.py:281
  54.1 10.6 %collective-permute-start.6 = (f32[4,128,128]{2,1,0:T(8,128)S(1)}, f32[4,128,128]{2,1,0:T(8,128)S(1)}, u32[]{:S(2)}, u32[]{:S(2)}) collective-permute-start(f32[4,128,128]{2,1,0:T(8,128)S(1)} %shard_map.76), channel_id=1, source_target_pairs={{0,16},{16,0},{1,17},{17,1},{2,18},{18,2},{3,19},{19,3},{4,20},{20... | collective-permute-start | bytes 786440 | tf_op jit(solution)/shard_map/ppermute | solution.py:281
  67.6 32.6 %all-to-all-start.1 = ((f32[16,48,128]{2,1,0:T(8,128)}), f32[16,48,128]{2,1,0:T(8,128)S(1)}, u32[]{:S(2)}, u32[]{:S(2)}) async-start(f32[16,48,128]{2,1,0:T(8,128)} %bitcast.10), calls=%async_computation.1 | async-start | bytes 786432 | tf_op jit(solution)/shard_map/all_to_all | solution.py:254
  79.4 49.1 %copy-start.3 = (f32[2,8,128,128]{3,2,1,0:T(8,128)S(1)}, f32[2,8,128,128]{3,2,1,0:T(8,128)}, u32[]{:S(2)}) copy-start(f32[2,8,128,128]{3,2,1,0:T(8,128)} %get-tuple-element.12.both_ref) | copy-start | bytes 3145732

commit v4 on v3

--- a/solution.py
+++ b/solution.py
@@ -20,6 +20,7 @@
 CAP = 384
 LINE = 4
 RING = 16
+PAIRS = 3
 f32, bf16 = jnp.float32, jnp.bfloat16
 LEFTS = dict(pack=(N, K), rows=(K, N), cols=(N, K), depth=(K, N), depth_t=(N, K))
 RIGHTS = dict(twice=(N, N), diag=(N, 2 * N))
@@ -114,10 +115,10 @@
 
 
 def forward(pair, store, lefts, rights):
-    first = right(pair.reshape(SLAB * N, N), right_table(rights, "twice"))
+    first = right(pair.reshape(-1, N), right_table(rights, "twice"))
     rows = left_table(lefts, "rows")
     lane = lax.broadcasted_iota(jnp.int32, (GRID, N), 1) < K
-    for z in range(0, SLAB, 2):
+    for z in range(0, pair.shape[0], 2):
         both = left(rows, jnp.concatenate([first[z * N : (z + 1) * N], first[(z + 1) * N : (z + 2) * N]], 1))
         for k in range(2):
             part = [both[low * GRID : (low + 1) * GRID, k * N : (k + 1) * N] for low in range(OWN)]
@@ -187,24 +188,37 @@
     out_ref[...] = jnp.where(step_ref[0] == 0, near[...], back[...])
 
 
-def pair_kernel(step_ref, psi_ref, one, two, near, far, back, swap, own_ref, lefts, rights, out_ref, occ_ref):
+def pair_store(out_ref, p, start):
+    def store(z, half, value):
+        out_ref[pl.ds((2 * p + half) * SLAB + start + z, GRID, stride=2 * PAIRS * SLAB), :] = value
+
+    return store
+
+
+def early_kernel(ids, psi_ref, two, one, near, back, own_ref, lefts, rights, kernel, out_ref, low_ref, high_ref, weight, sem):
     half = SLAB // 2
-    first, second = step_ref[0] == 0, step_ref[0] == 1
-    occ_ref[0, :half] = jnp.where(first, near[...], one[:half])
-    occ_ref[0, half:] = jnp.where(first, swap[...], one[half:])
-    occ_ref[1, :half] = jnp.where(first, far[...], jnp.where(second, swap[...], two[:half]))
-    occ_ref[1, half:] = jnp.where(first | second, back[...], two[half:])
-    count = occ_ref.shape[0]
-    blocks = 2 + 2 * count
+    step = ids[0]
+    copy = pltpu.make_async_copy(kernel.at[ids[1]], weight, sem)
+    copy.start()
+    low_ref[...] = jnp.where(step == 0, near[...], one[:half])
+    high_ref[...] = jnp.where(step < 2, back[...], two[half:])
     for k in range(2):
         for owner in range(GRID):
-            out_ref[pl.ds((owner * blocks + k) * SLAB, SLAB), :] = own_ref[pl.ds((owner * 2 + k) * SLAB, SLAB), :]
-    for p in range(count):
-
-        def store(z, half, value):
-            out_ref[pl.ds((2 + 2 * p + half) * SLAB + z, GRID, stride=blocks * SLAB), :] = value
-
-        forward(occ_ref[p] * psi_ref[...], store, lefts, rights)
+            to = pl.ds((owner * 2 * PAIRS + k) * SLAB, SLAB)
+            out_ref[to, :] = own_ref[pl.ds((owner * 2 + k) * SLAB, SLAB), :]
+    forward(low_ref[...] * psi_ref[:half], pair_store(out_ref, 1, 0), lefts, rights)
+    forward(high_ref[...] * psi_ref[half:], pair_store(out_ref, 2, half), lefts, rights)
+    copy.wait()
+
+
+def late_kernel(step_ref, psi_ref, two, one, far, swap, part_ref, lefts, rights, out_ref, low_ref, high_ref):
+    half = SLAB // 2
+    step = step_ref[0]
+    high_ref[...] = jnp.where(step == 0, swap[...], one[half:])
+    low_ref[...] = jnp.where(step == 0, far[...], jnp.where(step == 1, swap[...], two[:half]))
+    out_ref[...] = part_ref[...]
+    forward(high_ref[...] * psi_ref[half:], pair_store(out_ref, 1, half), lefts, rights)
+    forward(low_ref[...] * psi_ref[:half], pair_store(out_ref, 2, 0), lefts, rights)
 
 
 def pencil_kernel(in_ref, weight, lefts, out_ref):
@@ -216,19 +230,19 @@
             out_ref[:, 2 * p + half] = lines[:, half * N : (half + 1) * N].reshape(GRID, SLAB, N)
 
 
-def apply_kernel(in_ref, occ_ref, both_ref, lefts, rights, out_ref):
-    count = 1 + both_ref.shape[0]
-    blocks = in_ref.shape[0] // (GRID * SLAB)
-    for p in range(count):
+def apply_kernel(in_ref, occ_ref, low1, high1, low2, high2, lefts, rights, out_ref):
+    half = SLAB // 2
+    for p, (low, high) in enumerate(((occ_ref.at[:half], occ_ref.at[half:]), (low1, high1), (low2, high2))):
         spectrum = [
             jnp.concatenate(
-                [in_ref[pl.ds((2 * p + half) * SLAB + z, GRID, stride=blocks * SLAB), :] for z in range(SLAB)], 0
+                [in_ref[pl.ds((2 * p + side) * SLAB + z, GRID, stride=2 * PAIRS * SLAB), :] for z in range(SLAB)], 0
             )
-            for half in range(2)
+            for side in range(2)
         ]
         planes = backward(spectrum, lefts, rights)
         for z in range(SLAB):
-            out_ref[z] = out_ref[z] - both_ref[p - 1, z] * planes[z] if p else -occ_ref[z] * planes[z]
+            value = (low[z] if z < half else high[z - half]) * planes[z]
+            out_ref[z] = out_ref[z] - value if p else -value
 
 
 PARAMS = pltpu.CompilerParams(vmem_limit_bytes=50 * 2**20)
@@ -258,7 +272,6 @@
     lefts, rights, kernel = (jnp.asarray(table) for table in tables())
     grid_index = lax.axis_index("grid")
     index = grid_index.astype(jnp.int32).reshape(1)
-    weight = lax.dynamic_index_in_dim(kernel, grid_index, 0, keepdims=False)
     step = (lax.axis_index("band") % LINE).astype(jnp.int32).reshape(1)
     occ = occupied.reshape(SLAB, N, N)
     half = SLAB // 2
@@ -301,18 +314,26 @@
         (slab, slot_column.reshape(-1, N), occ, lefts, rights),
         scratch=(pltpu.VMEM((2 * N, GRID * CAP), bf16), pltpu.VMEM((OWN * K, GRID * CAP), bf16)),
     )
-    chosen = call(swap_kernel, (half, N, N), (step, near, back, far, psi), scalar=True, late=2)
+    chosen = call(swap_kernel, (half, N, N), (step, near, back, far, psi), scalar=True, late=2, flops=10**10)
     swap = send(chosen, {0: 1, 1: 0}, "stay")
-    sent, both = call(
-        pair_kernel,
-        [(6 * N, N), (2, SLAB, N, N)],
-        (step, psi, one, two, near, far, back, swap, sent, lefts, rights),
+    part, low1, high2, weight = call(
+        early_kernel,
+        [(2 * PAIRS * N, N), (half, N, N), (half, N, N), kernel.shape[1:]],
+        (jnp.concatenate([step, index]), psi, two, one, near, back, sent, lefts, rights, kernel),
         scalar=True,
-    )
-    got = exchange(sent.reshape(GRID, 6 * SLAB, N))
-    sent = call(pencil_kernel, (GRID, 6, SLAB, N), (got.reshape(GRID, 6, SLAB, N), weight, lefts))
-    got = exchange(sent.reshape(GRID, 6 * SLAB, N))
-    out = call(apply_kernel, (SLAB, N, N), (got.reshape(GRID * 6 * SLAB, N), occ, both, lefts, rights))
+        late=1,
+        scratch=(pltpu.SemaphoreType.DMA,),
+    )
+    sent, low2, high1 = call(
+        late_kernel,
+        [(2 * PAIRS * N, N), (half, N, N), (half, N, N)],
+        (step, psi, two, one, far, swap, part, lefts, rights),
+        scalar=True,
+    )
+    got = exchange(sent.reshape(GRID, 2 * PAIRS * SLAB, N)).reshape(GRID, 2 * PAIRS, SLAB, N)
+    sent = call(pencil_kernel, got.shape, (got, weight, lefts))
+    got = exchange(sent.reshape(GRID, 2 * PAIRS * SLAB, N)).reshape(-1, N)
+    out = call(apply_kernel, (SLAB, N, N), (got, occ, low1, high1, low2, high2, lefts, rights))
     return out.reshape(1, SLAB, N, N)
 
 

time: 131 us -> 130 us (level)
  blocking collectives: 27.6 us -> 60 us
  waiting for transfers between devices: 38.4 us -> 15 us
  starting transfers between devices: 49.4 us -> 38.3 us
  Pallas kernels: 12 us -> 13.6 us
    all_to_all x1 -> x2, blocking collectives: 27.6 us -> 60 us  [exchange(): lax.all_to_all(value, 'grid', split_axis=0, concat_axis=0, tiled=True)]
    all_to_all x2 -> x1, waiting for transfers between devices: 32.2 us -> 11.5 us  [exchange(): lax.all_to_all(value, 'grid', split_axis=0, concat_axis=0, tiled=True)]
    all_to_all x2 -> x1, starting transfers between devices: 25 us -> 14 us  [exchange(): lax.all_to_all(value, 'grid', split_axis=0, concat_axis=0, tiled=True)]
    ppermute x7, waiting for transfers between devices: 6.16 us -> 3.52 us  [send(): return lax.ppermute(value, ('band', 'grid'), pairs)]
    pallas_call x7 -> x8, Pallas kernels: 12 us -> 13.6 us  [call(): pl.pallas_call(kernel, out_shape=tuple((jax.ShapeDtypeStruct(s, f32) for...]
  transfers between devices with their start and end apart: 9 -> 8, of which waited for: 3 -> 2; matrix products, arithmetic and copies ran while one was open for 1% -> 0% of each run, Pallas kernels for 5% -> 7%
where the time goes in v4:
time: 130 us; the launch traced here: 129 us
  blocking collectives  60 us (46%)
  starting transfers between devices  38.3 us (29%)
  waiting for transfers between devices  15 us (12%)
  Pallas kernels  13.6 us (10%)
  local copies, waits for them, and re-layouts  1.86 us (1%)
    all_to_all x2, blocking collectives, exchange(): lax.all_to_all(value, 'grid', split_axis=0, concat_axis=0, tiled=True)  60 us
    ppermute x7, starting transfers between devices, send(): return lax.ppermute(value, ('band', 'grid'), pairs)  24.3 us
    all_to_all x1, starting transfers between devices, exchange(): lax.all_to_all(value, 'grid', split_axis=0, concat_axis=0, tiled=True)  14 us
    pallas_call x8, Pallas kernels, call(): pl.pallas_call(kernel, out_shape=tuple((jax.ShapeDtypeStruct(s, f32) for...  13.6 us
    all_to_all x1, waiting for transfers between devices, exchange(): lax.all_to_all(value, 'grid', split_axis=0, concat_axis=0, tiled=True)  11.5 us
    ppermute x7, waiting for transfers between devices, send(): return lax.ppermute(value, ('band', 'grid'), pairs)  3.52 us
  transfers between devices with their start and end apart: 8, of which 2 were waited for; matrix products, arithmetic and copies ran while one was open for 0% of the time, Pallas kernels for 7%

profile of v4, /device:TPU:1, one launch (start us, length us, event | category | flops | bytes accessed | tf_op | source)
XLA Modules:
  0.0 129.1 jit_solution(8826586308934065282)
XLA Ops:
  0.0 0.0 copy-start
  0.0 0.0 copy-start.4
  0.0 0.0 copy-start.5
  0.0 1.8 %slice_bitcast_fusion = (f32[4,128,128]{2,1,0:T(8,128)S(1)}, f32[4,128,128]{2,1,0:T(8,128)}) fusion(f32[1,8,128,128]{3,2,1,0:T(8,128)} %param.7), kind=kLoop, calls=%fused_computation | loop fusion | bytes 1048576 | tf_op jit(solution)/shard_map/slice | solution.py:298
  1.8 1.3 collective-permute-start.4
  3.1 1.3 %collective-permute-start.3 = (f32[4,128,128]{2,1,0:T(8,128)}, f32[4,128,128]{2,1,0:T(8,128)}, u32[]{:S(2)}, u32[]{:S(2)}) collective-permute-start(f32[4,128,128]{2,1,0:T(8,128)} %get-tuple-element.24), channel_id=1, source_target_pairs={{48,64},{49,65},{50,66},{51,67},{52,68},{53,69},{54,70},{55,71},{5... | collective-permute-start | bytes 786440 | tf_op jit(solution)/shard_map/ppermute | solution.py:294
  4.4 1.3 %collective-permute-start.2 = (f32[4,128,128]{2,1,0:T(8,128)}, f32[4,128,128]{2,1,0:T(8,128)}, u32[]{:S(2)}, u32[]{:S(2)}) collective-permute-start(f32[4,128,128]{2,1,0:T(8,128)} %get-tuple-element.24), channel_id=1, source_target_pairs={{32,64},{33,65},{34,66},{35,67},{36,68},{37,69},{38,70},{39,71},{4... | collective-permute-start | bytes 786440 | tf_op jit(solution)/shard_map/ppermute | solution.py:294
  5.7 0.0 copy-done
  5.7 0.0 copy-done.4
  5.7 0.0 copy-done.5
  5.8 0.9 shard_map.73.after
  6.6 14.0 %all-to-all-start = ((f32[16,8,384]{2,1,0:T(8,128)}), f32[16,8,384]{2,1,0:T(8,128)}, u32[]{:S(2)}, u32[]{:S(2)}) async-start(f32[16,8,384]{2,1,0:T(8,128)} %bitcast.4), calls=%async_computation | async-start | bytes 393216 | tf_op jit(solution)/shard_map/all_to_all | solution.py:268
  20.7 0.0 collective-permute-done.4.value
  20.7 0.0 copy-start.2
  20.7 0.0 copy-start.1
  20.7 0.0 copy-start.6
  20.8 9.4 %collective-permute-start.5 = (f32[4,128,128]{2,1,0:T(8,128)S(1)}, f32[4,128,128]{2,1,0:T(8,128)S(1)}, u32[]{:S(2)}, u32[]{:S(2)}) collective-permute-start(f32[4,128,128]{2,1,0:T(8,128)S(1)} %shard_map.75), channel_id=1, source_target_pairs={{2,80},{18,64},{79,81},{95,65},{4,82},{20,66},{1,83},{17,67},{6,84... | collective-permute-start | bytes 786440 | tf_op jit(solution)/shard_map/ppermute | solution.py:294
  30.1 0.0 copy-done.2
  30.1 2.0 %collective-permute-start.1 = (f32[8,128,128]{2,1,0:T(8,128)S(1)}, f32[8,128,128]{2,1,0:T(8,128)S(1)}, u32[]{:S(2)}, u32[]{:S(2)}) collective-permute-start(f32[8,128,128]{2,1,0:T(8,128)S(1)} %bitcast.17), channel_id=1, source_target_pairs={{0,16},{16,32},{32,48},{1,17},{17,33},{33,49},{2,18},{18,34},{34,5... | collective-permute-start | bytes 1572872 | tf_op jit(solution)/shard_map/ppermute | solution.py:294
  32.2 4.6 %collective-permute-start = (f32[8,128,128]{2,1,0:T(8,128)S(1)}, f32[8,128,128]{2,1,0:T(8,128)S(1)}, u32[]{:S(2)}, u32[]{:S(2)}) collective-permute-start(f32[8,128,128]{2,1,0:T(8,128)S(1)} %bitcast.18), channel_id=1, source_target_pairs={{0,32},{16,48},{1,33},{17,49},{2,34},{18,50},{3,35},{19,51},{4,36}... | collective-permute-start | bytes 1572872 | tf_op jit(solution)/shard_map/ppermute | solution.py:294
  36.8 11.5 %all-to-all-done = f32[16,8,384]{2,1,0:T(8,128)} async-done(((f32[16,8,384]{2,1,0:T(8,128)}), f32[16,8,384]{2,1,0:T(8,128)}, u32[]{:S(2)}, u32[]{:S(2)}) %all-to-all-start) | async-done | bytes 196640 | tf_op jit(solution)/shard_map/all_to_all | solution.py:268
  48.3 0.0 copy-done.1
  48.3 0.0 copy-done.6
  48.3 4.8 %shard_map.74 = (f32[8,128,128]{2,1,0:T(8,128)S(1)}, f32[256,128]{1,0:T(8,128)S(1)}) custom-call(f32[128,384]{1,0:T(8,128)} %bitcast.5.slab_ref, s32[48,128]{1,0:T(8,128)S(1)} %bitcast.27, f32[8,128,128]{2,1,0:T(8,128)S(1)} %bitcast.19, bf16[512,384]{1,0:T(8,128)(2,1)S(1)} %copy-done, bf16[768,256]{1,0:T(8,128)(2,1)S(1)} %copy-done.1), custom_call_target="tpu_custom_call" | custom-call | flops 1 | bytes 1 | tf_op jit(solution)/shard_map/pallas_call | solution.py:256
  53.1 0.0 collective-permute-done.3.near
  53.1 0.0 collective-permute-done.2.after.far
  53.1 0.0 collective-permute-done.5.back
  53.1 1.0 shard_map.76
  54.1 4.4 %collective-permute-start.6 = (f32[4,128,128]{2,1,0:T(8,128)S(1)}, f32[4,128,128]{2,1,0:T(8,128)S(1)}, u32[]{:S(2)}, u32[]{:S(2)}) collective-permute-start(f32[4,128,128]{2,1,0:T(8,128)S(1)} %shard_map.76), channel_id=1, source_target_pairs={{0,16},{16,0},{1,17},{17,1},{2,18},{18,2},{3,19},{19,3},{4,20},{20... | collective-permute-start | bytes 786440 | tf_op jit(solution)/shard_map/ppermute | solution.py:294
  58.5 0.1 pad_add_fusion.ids
  58.6 0.0 collective-permute-done.1.one
  58.6 0.0 copy-start.3
  58.6 0.0 collective-permute-done.two
  58.6 2.6 %shard_map.77 = (f32[768,128]{1,0:T(8,128)S(1)}, f32[4,128,128]{2,1,0:T(8,128)S(1)}, f32[4,128,128]{2,1,0:T(8,128)S(1)}, f32[64,256]{1,0:T(8,128)S(1)}) custom-call(s32[2]{0:T(128)S(1)} %pad_add_fusion.ids, f32[8,128,128]{2,1,0:T(8,128)S(1)} %get-tuple-element.14.also.psi_ref, f32[8,128,128]{2,1,0:T(8,128)S(1)} %collective-permute-done.two, ...), custom_call_target="tpu_custom_call" | custom-call | flops 1 | bytes 1 | tf_op jit(solution)/shard_map/pallas_call | solution.py:256
  61.2 0.0 copy-done.3
  61.2 3.5 %collective-permute-done.6.swap = f32[4,128,128]{2,1,0:T(8,128)S(1)} collective-permute-done((f32[4,128,128]{2,1,0:T(8,128)S(1)}, f32[4,128,128]{2,1,0:T(8,128)S(1)}, u32[]{:S(2)}, u32[]{:S(2)}) %collective-permute-start.6) | collective-permute-done | bytes 262176 | tf_op jit(solution)/shard_map/ppermute | solution.py:294
  64.7 1.8 %shard_map.78 = (f32[768,128]{1,0:T(8,128)S(1)}, f32[4,128,128]{2,1,0:T(8,128)S(1)}, f32[4,128,128]{2,1,0:T(8,128)S(1)}) custom-call(s32[1]{0:T(128)} %bitcast.step_ref, f32[8,128,128]{2,1,0:T(8,128)S(1)} %get-tuple-element.14.also.psi_ref, f32[8,128,128]{2,1,0:T(8,128)S(1)} %collective-permute-done.two, f32[8,128,128]{2,1,0:T(8,128)} %copy-done.3, ...), custom_call_target="tpu_custom_call" | custom-call | flops 1 | bytes 1 | tf_op jit(solution)/shard_map/pallas_call | solution.py:256
  66.5 32.5 %all_to_all.15 = f32[16,48,128]{2,1,0:T(8,128)S(1)} all-to-all(f32[16,48,128]{2,1,0:T(8,128)S(1)} %bitcast.24), channel_id=1, replica_groups=mesh['band'=32,'grid'=16] {'grid'}, dimensions={0} | all-to-all | bytes 786432 | tf_op jit(solution)/shard_map/all_to_all | solution.py:268
  99.0 0.7 shard_map.79
  99.7 27.6 %all_to_all.16 = f32[16,48,128]{2,1,0:T(8,128)S(1)} all-to-all(f32[16,48,128]{2,1,0:T(8,128)S(1)} %bitcast.23), channel_id=1, replica_groups=mesh['band'=32,'grid'=16] {'grid'}, dimensions={0} | all-to-all | bytes 786432 | tf_op jit(solution)/shard_map/all_to_all | solution.py:268
  127.3 1.8 %shard_map.80 = f32[8,128,128]{2,1,0:T(8,128)} custom-call(f32[768,128]{1,0:T(8,128)S(1)} %bitcast.21, f32[8,128,128]{2,1,0:T(8,128)S(1)} %bitcast.20, f32[4,128,128]{2,1,0:T(8,128)S(1)} %get-tuple-element.19.low1, f32[4,128,128]{2,1,0:T(8,128)S(1)} %get-tuple-element.20.high1, f32[4,128,128]{2,1,0:T(8,128)S(1)} %get-tuple-element.21.low2, ...), custom_call_target="tpu_custom_call" | custom-call | flops 1 | bytes 1 | tf_op jit(solution)/shard_map/pallas_call | solution.py:256
  (1 shorter events, 0.0 us)
Async XLA Ops:
  0.0 5.7 %copy-start = (bf16[512,384]{1,0:T(8,128)(2,1)S(1)}, bf16[512,384]{1,0:T(8,128)(2,1)}, u32[]{:S(2)}) copy-start(bf16[512,384]{1,0:T(8,128)(2,1)} %constant.28.clone.lefts) | copy-start | bytes 1179652
  0.0 5.7 %copy-start.4 = (f32[1,64,384]{2,1,0:T(8,128)S(1)}, f32[1,64,384]{2,1,0:T(8,128)}, u32[]{:S(2)}) copy-start(f32[1,64,384]{2,1,0:T(8,128)} %param.8) | copy-start | bytes 294916
  0.0 5.7 %copy-start.5 = (s32[6144]{0:T(1024)S(1)}, s32[6144]{0:T(1024)}, u32[]{:S(2)}) copy-start(s32[6144]{0:T(1024)} %param.10) | copy-start | bytes 73732
  1.8 18.9 %collective-permute-start.4 = (f32[4,128,128]{2,1,0:T(8,128)S(1)}, f32[4,128,128]{2,1,0:T(8,128)S(1)}, u32[]{:S(2)}, u32[]{:S(2)}) collective-permute-start(f32[4,128,128]{2,1,0:T(8,128)S(1)} %get-tuple-element.23), channel_id=1, source_target_pairs={{48,2},{32,18},{49,79},{33,95},{50,4},{34,20},{51,1},{35,17},{52,6... | collective-permute-start | bytes 786440 | tf_op jit(solution)/shard_map/ppermute | solution.py:294
  3.1 50.0 %collective-permute-start.3 = (f32[4,128,128]{2,1,0:T(8,128)}, f32[4,128,128]{2,1,0:T(8,128)}, u32[]{:S(2)}, u32[]{:S(2)}) collective-permute-start(f32[4,128,128]{2,1,0:T(8,128)} %get-tuple-element.24), channel_id=1, source_target_pairs={{48,64},{49,65},{50,66},{51,67},{52,68},{53,69},{54,70},{55,71},{5... | collective-permute-start | bytes 786440 | tf_op jit(solution)/shard_map/ppermute | solution.py:294
  4.4 48.7 %collective-permute-start.2 = (f32[4,128,128]{2,1,0:T(8,128)}, f32[4,128,128]{2,1,0:T(8,128)}, u32[]{:S(2)}, u32[]{:S(2)}) collective-permute-start(f32[4,128,128]{2,1,0:T(8,128)} %get-tuple-element.24), channel_id=1, source_target_pairs={{32,64},{33,65},{34,66},{35,67},{36,68},{37,69},{38,70},{39,71},{4... | collective-permute-start | bytes 786440 | tf_op jit(solution)/shard_map/ppermute | solution.py:294
  6.6 41.7 %all-to-all-start = ((f32[16,8,384]{2,1,0:T(8,128)}), f32[16,8,384]{2,1,0:T(8,128)}, u32[]{:S(2)}, u32[]{:S(2)}) async-start(f32[16,8,384]{2,1,0:T(8,128)} %bitcast.4), calls=%async_computation | async-start | bytes 393216 | tf_op jit(solution)/shard_map/all_to_all | solution.py:268
  20.7 9.4 %copy-start.2 = (f32[1,8,128,128]{3,2,1,0:T(8,128)S(1)}, f32[1,8,128,128]{3,2,1,0:T(8,128)}, u32[]{:S(2)}) copy-start(f32[1,8,128,128]{3,2,1,0:T(8,128)} %param.7) | copy-start | bytes 1572868
  20.7 27.6 %copy-start.1 = (bf16[768,256]{1,0:T(8,128)(2,1)S(1)}, bf16[768,256]{1,0:T(8,128)(2,1)}, u32[]{:S(2)}) copy-start(bf16[768,256]{1,0:T(8,128)(2,1)} %constant.29.clone.rights) | copy-start | bytes 1179652
  20.7 27.6 %copy-start.6 = (s32[6144]{0:T(1024)S(1)}, s32[6144]{0:T(1024)}, u32[]{:S(2)}) copy-start(s32[6144]{0:T(1024)} %param.9) | copy-start | bytes 73732
  20.8 32.4 %collective-permute-start.5 = (f32[4,128,128]{2,1,0:T(8,128)S(1)}, f32[4,128,128]{2,1,0:T(8,128)S(1)}, u32[]{:S(2)}, u32[]{:S(2)}) collective-permute-start(f32[4,128,128]{2,1,0:T(8,128)S(1)} %shard_map.75), channel_id=1, source_target_pairs={{2,80},{18,64},{79,81},{95,65},{4,82},{20,66},{1,83},{17,67},{6,84... | collective-permute-start | bytes 786440 | tf_op jit(solution)/shard_map/ppermute | solution.py:294
  30.1 28.4 %collective-permute-start.1 = (f32[8,128,128]{2,1,0:T(8,128)S(1)}, f32[8,128,128]{2,1,0:T(8,128)S(1)}, u32[]{:S(2)}, u32[]{:S(2)}) collective-permute-start(f32[8,128,128]{2,1,0:T(8,128)S(1)} %bitcast.17), channel_id=1, source_target_pairs={{0,16},{16,32},{32,48},{1,17},{17,33},{33,49},{2,18},{18,34},{34,5... | collective-permute-start | bytes 1572872 | tf_op jit(solution)/shard_map/ppermute | solution.py:294
  32.2 26.4 %collective-permute-start = (f32[8,128,128]{2,1,0:T(8,128)S(1)}, f32[8,128,128]{2,1,0:T(8,128)S(1)}, u32[]{:S(2)}, u32[]{:S(2)}) collective-permute-start(f32[8,128,128]{2,1,0:T(8,128)S(1)} %bitcast.18), channel_id=1, source_target_pairs={{0,32},{16,48},{1,33},{17,49},{2,34},{18,50},{3,35},{19,51},{4,36}... | collective-permute-start | bytes 1572872 | tf_op jit(solution)/shard_map/ppermute | solution.py:294
  54.1 10.6 %collective-permute-start.6 = (f32[4,128,128]{2,1,0:T(8,128)S(1)}, f32[4,128,128]{2,1,0:T(8,128)S(1)}, u32[]{:S(2)}, u32[]{:S(2)}) collective-permute-start(f32[4,128,128]{2,1,0:T(8,128)S(1)} %shard_map.76), channel_id=1, source_target_pairs={{0,16},{16,0},{1,17},{17,1},{2,18},{18,2},{3,19},{19,3},{4,20},{20... | collective-permute-start | bytes 786440 | tf_op jit(solution)/shard_map/ppermute | solution.py:294
  58.6 2.6 %copy-start.3 = (f32[8,128,128]{2,1,0:T(8,128)}, f32[8,128,128]{2,1,0:T(8,128)S(1)}, u32[]{:S(2)}) copy-start(f32[8,128,128]{2,1,0:T(8,128)S(1)} %collective-permute-done.1.one) | copy-start | bytes 1572868

commit v5 on v4

--- a/solution.py
+++ b/solution.py
@@ -245,12 +245,12 @@
             out_ref[z] = out_ref[z] - value if p else -value
 
 
-PARAMS = pltpu.CompilerParams(vmem_limit_bytes=50 * 2**20)
+GRANT = 50
 VM = pl.BlockSpec(memory_space=pltpu.VMEM)
 SM = pl.BlockSpec(memory_space=pltpu.SMEM)
 
 
-def call(kernel, shapes, ins, scalar=False, late=0, flops=1, scratch=()):
+def call(kernel, shapes, ins, scalar=False, late=0, flops=1, grant=GRANT, scratch=()):
     many = isinstance(shapes, list)
     specs = [SM if scalar and k == 0 else VM for k in range(len(ins) - late)]
     return pl.pallas_call(
@@ -259,7 +259,7 @@
         in_specs=specs + [pl.BlockSpec(memory_space=pl.ANY)] * late,
         out_specs=tuple(VM for _ in shapes) if many else VM,
         scratch_shapes=scratch,
-        compiler_params=PARAMS,
+        compiler_params=pltpu.CompilerParams(vmem_limit_bytes=grant * 2**20),
         cost_estimate=pl.CostEstimate(flops=flops, bytes_accessed=1, transcendentals=0),
     )(*ins)
 
@@ -314,7 +314,7 @@
         (slab, slot_column.reshape(-1, N), occ, lefts, rights),
         scratch=(pltpu.VMEM((2 * N, GRID * CAP), bf16), pltpu.VMEM((OWN * K, GRID * CAP), bf16)),
     )
-    chosen = call(swap_kernel, (half, N, N), (step, near, back, far, psi), scalar=True, late=2, flops=10**10)
+    chosen = call(swap_kernel, (half, N, N), (step, near, back, far, psi), scalar=True, late=2, flops=10**10, grant=8)
     swap = send(chosen, {0: 1, 1: 0}, "stay")
     part, low1, high2, weight = call(
         early_kernel,

time: 130 us -> 130 us (level)
  no operation moved by 1% of the time
where the time goes in v5:
time: 130 us; the launch traced here: 129 us
  blocking collectives  60 us (46%)
  starting transfers between devices  38.3 us (29%)
  waiting for transfers between devices  15 us (12%)
  Pallas kernels  13.6 us (10%)
  local copies, waits for them, and re-layouts  1.86 us (1%)
    all_to_all x2, blocking collectives, exchange(): lax.all_to_all(value, 'grid', split_axis=0, concat_axis=0, tiled=True)  60 us
    ppermute x7, starting transfers between devices, send(): return lax.ppermute(value, ('band', 'grid'), pairs)  24.3 us
    all_to_all x1, starting transfers between devices, exchange(): lax.all_to_all(value, 'grid', split_axis=0, concat_axis=0, tiled=True)  14 us
    pallas_call x8, Pallas kernels, call(): pl.pallas_call(kernel, out_shape=tuple((jax.ShapeDtypeStruct(s, f32) for...  13.6 us
    all_to_all x1, waiting for transfers between devices, exchange(): lax.all_to_all(value, 'grid', split_axis=0, concat_axis=0, tiled=True)  11.5 us
    ppermute x7, waiting for transfers between devices, send(): return lax.ppermute(value, ('band', 'grid'), pairs)  3.52 us
  transfers between devices with their start and end apart: 8, of which 2 were waited for; matrix products, arithmetic and copies ran while one was open for 0% of the time, Pallas kernels for 7%

profile of v5, /device:TPU:1, one launch (start us, length us, event | category | flops | bytes accessed | tf_op | source)
XLA Modules:
  0.0 129.1 jit_solution(3659359275464930476)
XLA Ops:
  0.0 0.0 copy-start
  0.0 0.0 copy-start.4
  0.0 0.0 copy-start.5
  0.0 1.8 %slice_bitcast_fusion = (f32[4,128,128]{2,1,0:T(8,128)S(1)}, f32[4,128,128]{2,1,0:T(8,128)}) fusion(f32[1,8,128,128]{3,2,1,0:T(8,128)} %param.7), kind=kLoop, calls=%fused_computation | loop fusion | bytes 1048576 | tf_op jit(solution)/shard_map/slice | solution.py:298
  1.8 1.3 collective-permute-start.4
  3.1 1.3 %collective-permute-start.3 = (f32[4,128,128]{2,1,0:T(8,128)}, f32[4,128,128]{2,1,0:T(8,128)}, u32[]{:S(2)}, u32[]{:S(2)}) collective-permute-start(f32[4,128,128]{2,1,0:T(8,128)} %get-tuple-element.24), channel_id=1, source_target_pairs={{48,64},{49,65},{50,66},{51,67},{52,68},{53,69},{54,70},{55,71},{5... | collective-permute-start | bytes 786440 | tf_op jit(solution)/shard_map/ppermute | solution.py:294
  4.4 1.3 %collective-permute-start.2 = (f32[4,128,128]{2,1,0:T(8,128)}, f32[4,128,128]{2,1,0:T(8,128)}, u32[]{:S(2)}, u32[]{:S(2)}) collective-permute-start(f32[4,128,128]{2,1,0:T(8,128)} %get-tuple-element.24), channel_id=1, source_target_pairs={{32,64},{33,65},{34,66},{35,67},{36,68},{37,69},{38,70},{39,71},{4... | collective-permute-start | bytes 786440 | tf_op jit(solution)/shard_map/ppermute | solution.py:294
  5.7 0.0 copy-done
  5.7 0.0 copy-done.4
  5.7 0.0 copy-done.5
  5.8 0.9 shard_map.73.after
  6.6 14.0 %all-to-all-start = ((f32[16,8,384]{2,1,0:T(8,128)}), f32[16,8,384]{2,1,0:T(8,128)}, u32[]{:S(2)}, u32[]{:S(2)}) async-start(f32[16,8,384]{2,1,0:T(8,128)} %bitcast.4), calls=%async_computation | async-start | bytes 393216 | tf_op jit(solution)/shard_map/all_to_all | solution.py:268
  20.7 0.0 collective-permute-done.4.value
  20.7 0.0 copy-start.2
  20.7 0.0 copy-start.1
  20.7 0.0 copy-start.6
  20.8 9.4 %collective-permute-start.5 = (f32[4,128,128]{2,1,0:T(8,128)S(1)}, f32[4,128,128]{2,1,0:T(8,128)S(1)}, u32[]{:S(2)}, u32[]{:S(2)}) collective-permute-start(f32[4,128,128]{2,1,0:T(8,128)S(1)} %shard_map.75), channel_id=1, source_target_pairs={{2,80},{18,64},{79,81},{95,65},{4,82},{20,66},{1,83},{17,67},{6,84... | collective-permute-start | bytes 786440 | tf_op jit(solution)/shard_map/ppermute | solution.py:294
  30.1 0.0 copy-done.2
  30.1 2.0 %collective-permute-start.1 = (f32[8,128,128]{2,1,0:T(8,128)S(1)}, f32[8,128,128]{2,1,0:T(8,128)S(1)}, u32[]{:S(2)}, u32[]{:S(2)}) collective-permute-start(f32[8,128,128]{2,1,0:T(8,128)S(1)} %bitcast.17), channel_id=1, source_target_pairs={{0,16},{16,32},{32,48},{1,17},{17,33},{33,49},{2,18},{18,34},{34,5... | collective-permute-start | bytes 1572872 | tf_op jit(solution)/shard_map/ppermute | solution.py:294
  32.2 4.6 %collective-permute-start = (f32[8,128,128]{2,1,0:T(8,128)S(1)}, f32[8,128,128]{2,1,0:T(8,128)S(1)}, u32[]{:S(2)}, u32[]{:S(2)}) collective-permute-start(f32[8,128,128]{2,1,0:T(8,128)S(1)} %bitcast.18), channel_id=1, source_target_pairs={{0,32},{16,48},{1,33},{17,49},{2,34},{18,50},{3,35},{19,51},{4,36}... | collective-permute-start | bytes 1572872 | tf_op jit(solution)/shard_map/ppermute | solution.py:294
  36.8 11.5 %all-to-all-done = f32[16,8,384]{2,1,0:T(8,128)} async-done(((f32[16,8,384]{2,1,0:T(8,128)}), f32[16,8,384]{2,1,0:T(8,128)}, u32[]{:S(2)}, u32[]{:S(2)}) %all-to-all-start) | async-done | bytes 196640 | tf_op jit(solution)/shard_map/all_to_all | solution.py:268
  48.3 0.0 copy-done.1
  48.3 0.0 copy-done.6
  48.3 4.8 %shard_map.74 = (f32[8,128,128]{2,1,0:T(8,128)S(1)}, f32[256,128]{1,0:T(8,128)S(1)}) custom-call(f32[128,384]{1,0:T(8,128)} %bitcast.5.slab_ref, s32[48,128]{1,0:T(8,128)S(1)} %bitcast.27, f32[8,128,128]{2,1,0:T(8,128)S(1)} %bitcast.19, bf16[512,384]{1,0:T(8,128)(2,1)S(1)} %copy-done, bf16[768,256]{1,0:T(8,128)(2,1)S(1)} %copy-done.1), custom_call_target="tpu_custom_call" | custom-call | flops 1 | bytes 1 | tf_op jit(solution)/shard_map/pallas_call | solution.py:256
  53.1 0.0 collective-permute-done.3.near
  53.1 0.0 collective-permute-done.2.after.far
  53.1 0.0 collective-permute-done.5.back
  53.1 1.0 shard_map.76
  54.1 4.4 %collective-permute-start.6 = (f32[4,128,128]{2,1,0:T(8,128)S(1)}, f32[4,128,128]{2,1,0:T(8,128)S(1)}, u32[]{:S(2)}, u32[]{:S(2)}) collective-permute-start(f32[4,128,128]{2,1,0:T(8,128)S(1)} %shard_map.76), channel_id=1, source_target_pairs={{0,16},{16,0},{1,17},{17,1},{2,18},{18,2},{3,19},{19,3},{4,20},{20... | collective-permute-start | bytes 786440 | tf_op jit(solution)/shard_map/ppermute | solution.py:294
  58.5 0.1 pad_add_fusion.ids
  58.6 0.0 collective-permute-done.1.one
  58.6 0.0 copy-start.3
  58.6 0.0 collective-permute-done.two
  58.6 2.6 %shard_map.77 = (f32[768,128]{1,0:T(8,128)S(1)}, f32[4,128,128]{2,1,0:T(8,128)S(1)}, f32[4,128,128]{2,1,0:T(8,128)S(1)}, f32[64,256]{1,0:T(8,128)S(1)}) custom-call(s32[2]{0:T(128)S(1)} %pad_add_fusion.ids, f32[8,128,128]{2,1,0:T(8,128)S(1)} %get-tuple-element.14.also.psi_ref, f32[8,128,128]{2,1,0:T(8,128)S(1)} %collective-permute-done.two, ...), custom_call_target="tpu_custom_call" | custom-call | flops 1 | bytes 1 | tf_op jit(solution)/shard_map/pallas_call | solution.py:256
  61.2 0.0 copy-done.3
  61.2 3.5 %collective-permute-done.6.swap = f32[4,128,128]{2,1,0:T(8,128)S(1)} collective-permute-done((f32[4,128,128]{2,1,0:T(8,128)S(1)}, f32[4,128,128]{2,1,0:T(8,128)S(1)}, u32[]{:S(2)}, u32[]{:S(2)}) %collective-permute-start.6) | collective-permute-done | bytes 262176 | tf_op jit(solution)/shard_map/ppermute | solution.py:294
  64.7 1.8 %shard_map.78 = (f32[768,128]{1,0:T(8,128)S(1)}, f32[4,128,128]{2,1,0:T(8,128)S(1)}, f32[4,128,128]{2,1,0:T(8,128)S(1)}) custom-call(s32[1]{0:T(128)} %bitcast.step_ref, f32[8,128,128]{2,1,0:T(8,128)S(1)} %get-tuple-element.14.also.psi_ref, f32[8,128,128]{2,1,0:T(8,128)S(1)} %collective-permute-done.two, f32[8,128,128]{2,1,0:T(8,128)} %copy-done.3, ...), custom_call_target="tpu_custom_call" | custom-call | flops 1 | bytes 1 | tf_op jit(solution)/shard_map/pallas_call | solution.py:256
  66.5 32.5 %all_to_all.15 = f32[16,48,128]{2,1,0:T(8,128)S(1)} all-to-all(f32[16,48,128]{2,1,0:T(8,128)S(1)} %bitcast.24), channel_id=1, replica_groups=mesh['band'=32,'grid'=16] {'grid'}, dimensions={0} | all-to-all | bytes 786432 | tf_op jit(solution)/shard_map/all_to_all | solution.py:268
  99.0 0.7 shard_map.79
  99.7 27.6 %all_to_all.16 = f32[16,48,128]{2,1,0:T(8,128)S(1)} all-to-all(f32[16,48,128]{2,1,0:T(8,128)S(1)} %bitcast.23), channel_id=1, replica_groups=mesh['band'=32,'grid'=16] {'grid'}, dimensions={0} | all-to-all | bytes 786432 | tf_op jit(solution)/shard_map/all_to_all | solution.py:268
  127.3 1.8 %shard_map.80 = f32[8,128,128]{2,1,0:T(8,128)} custom-call(f32[768,128]{1,0:T(8,128)S(1)} %bitcast.21, f32[8,128,128]{2,1,0:T(8,128)S(1)} %bitcast.20, f32[4,128,128]{2,1,0:T(8,128)S(1)} %get-tuple-element.19.low1, f32[4,128,128]{2,1,0:T(8,128)S(1)} %get-tuple-element.20.high1, f32[4,128,128]{2,1,0:T(8,128)S(1)} %get-tuple-element.21.low2, ...), custom_call_target="tpu_custom_call" | custom-call | flops 1 | bytes 1 | tf_op jit(solution)/shard_map/pallas_call | solution.py:256
  (1 shorter events, 0.0 us)
Async XLA Ops:
  0.0 5.7 %copy-start = (bf16[512,384]{1,0:T(8,128)(2,1)S(1)}, bf16[512,384]{1,0:T(8,128)(2,1)}, u32[]{:S(2)}) copy-start(bf16[512,384]{1,0:T(8,128)(2,1)} %constant.28.clone.lefts) | copy-start | bytes 1179652
  0.0 5.7 %copy-start.4 = (f32[1,64,384]{2,1,0:T(8,128)S(1)}, f32[1,64,384]{2,1,0:T(8,128)}, u32[]{:S(2)}) copy-start(f32[1,64,384]{2,1,0:T(8,128)} %param.8) | copy-start | bytes 294916
  0.0 5.7 %copy-start.5 = (s32[6144]{0:T(1024)S(1)}, s32[6144]{0:T(1024)}, u32[]{:S(2)}) copy-start(s32[6144]{0:T(1024)} %param.10) | copy-start | bytes 73732
  1.8 18.9 %collective-permute-start.4 = (f32[4,128,128]{2,1,0:T(8,128)S(1)}, f32[4,128,128]{2,1,0:T(8,128)S(1)}, u32[]{:S(2)}, u32[]{:S(2)}) collective-permute-start(f32[4,128,128]{2,1,0:T(8,128)S(1)} %get-tuple-element.23), channel_id=1, source_target_pairs={{48,2},{32,18},{49,79},{33,95},{50,4},{34,20},{51,1},{35,17},{52,6... | collective-permute-start | bytes 786440 | tf_op jit(solution)/shard_map/ppermute | solution.py:294
  3.1 50.0 %collective-permute-start.3 = (f32[4,128,128]{2,1,0:T(8,128)}, f32[4,128,128]{2,1,0:T(8,128)}, u32[]{:S(2)}, u32[]{:S(2)}) collective-permute-start(f32[4,128,128]{2,1,0:T(8,128)} %get-tuple-element.24), channel_id=1, source_target_pairs={{48,64},{49,65},{50,66},{51,67},{52,68},{53,69},{54,70},{55,71},{5... | collective-permute-start | bytes 786440 | tf_op jit(solution)/shard_map/ppermute | solution.py:294
  4.4 48.7 %collective-permute-start.2 = (f32[4,128,128]{2,1,0:T(8,128)}, f32[4,128,128]{2,1,0:T(8,128)}, u32[]{:S(2)}, u32[]{:S(2)}) collective-permute-start(f32[4,128,128]{2,1,0:T(8,128)} %get-tuple-element.24), channel_id=1, source_target_pairs={{32,64},{33,65},{34,66},{35,67},{36,68},{37,69},{38,70},{39,71},{4... | collective-permute-start | bytes 786440 | tf_op jit(solution)/shard_map/ppermute | solution.py:294
  6.6 41.7 %all-to-all-start = ((f32[16,8,384]{2,1,0:T(8,128)}), f32[16,8,384]{2,1,0:T(8,128)}, u32[]{:S(2)}, u32[]{:S(2)}) async-start(f32[16,8,384]{2,1,0:T(8,128)} %bitcast.4), calls=%async_computation | async-start | bytes 393216 | tf_op jit(solution)/shard_map/all_to_all | solution.py:268
  20.7 9.4 %copy-start.2 = (f32[1,8,128,128]{3,2,1,0:T(8,128)S(1)}, f32[1,8,128,128]{3,2,1,0:T(8,128)}, u32[]{:S(2)}) copy-start(f32[1,8,128,128]{3,2,1,0:T(8,128)} %param.7) | copy-start | bytes 1572868
  20.7 27.6 %copy-start.1 = (bf16[768,256]{1,0:T(8,128)(2,1)S(1)}, bf16[768,256]{1,0:T(8,128)(2,1)}, u32[]{:S(2)}) copy-start(bf16[768,256]{1,0:T(8,128)(2,1)} %constant.29.clone.rights) | copy-start | bytes 1179652
  20.7 27.6 %copy-start.6 = (s32[6144]{0:T(1024)S(1)}, s32[6144]{0:T(1024)}, u32[]{:S(2)}) copy-start(s32[6144]{0:T(1024)} %param.9) | copy-start | bytes 73732
  20.8 32.4 %collective-permute-start.5 = (f32[4,128,128]{2,1,0:T(8,128)S(1)}, f32[4,128,128]{2,1,0:T(8,128)S(1)}, u32[]{:S(2)}, u32[]{:S(2)}) collective-permute-start(f32[4,128,128]{2,1,0:T(8,128)S(1)} %shard_map.75), channel_id=1, source_target_pairs={{2,80},{18,64},{79,81},{95,65},{4,82},{20,66},{1,83},{17,67},{6,84... | collective-permute-start | bytes 786440 | tf_op jit(solution)/shard_map/ppermute | solution.py:294
  30.1 28.4 %collective-permute-start.1 = (f32[8,128,128]{2,1,0:T(8,128)S(1)}, f32[8,128,128]{2,1,0:T(8,128)S(1)}, u32[]{:S(2)}, u32[]{:S(2)}) collective-permute-start(f32[8,128,128]{2,1,0:T(8,128)S(1)} %bitcast.17), channel_id=1, source_target_pairs={{0,16},{16,32},{32,48},{1,17},{17,33},{33,49},{2,18},{18,34},{34,5... | collective-permute-start | bytes 1572872 | tf_op jit(solution)/shard_map/ppermute | solution.py:294
  32.2 26.4 %collective-permute-start = (f32[8,128,128]{2,1,0:T(8,128)S(1)}, f32[8,128,128]{2,1,0:T(8,128)S(1)}, u32[]{:S(2)}, u32[]{:S(2)}) collective-permute-start(f32[8,128,128]{2,1,0:T(8,128)S(1)} %bitcast.18), channel_id=1, source_target_pairs={{0,32},{16,48},{1,33},{17,49},{2,34},{18,50},{3,35},{19,51},{4,36}... | collective-permute-start | bytes 1572872 | tf_op jit(solution)/shard_map/ppermute | solution.py:294
  54.1 10.6 %collective-permute-start.6 = (f32[4,128,128]{2,1,0:T(8,128)S(1)}, f32[4,128,128]{2,1,0:T(8,128)S(1)}, u32[]{:S(2)}, u32[]{:S(2)}) collective-permute-start(f32[4,128,128]{2,1,0:T(8,128)S(1)} %shard_map.76), channel_id=1, source_target_pairs={{0,16},{16,0},{1,17},{17,1},{2,18},{18,2},{3,19},{19,3},{4,20},{20... | collective-permute-start | bytes 786440 | tf_op jit(solution)/shard_map/ppermute | solution.py:294
  58.6 2.6 %copy-start.3 = (f32[8,128,128]{2,1,0:T(8,128)}, f32[8,128,128]{2,1,0:T(8,128)S(1)}, u32[]{:S(2)}) copy-start(f32[8,128,128]{2,1,0:T(8,128)S(1)} %collective-permute-done.1.one) | copy-start | bytes 1572868
